TPU v7x, 1024 devices: a whole 8x8x8 slice. The times are simulated.
1024 devices in a mesh: region: 128 (over y_lo, x, z), group: 8 (over y_hi, core).
Axes of the slice: x: 8, y: 8 (y_hi: 4, y_lo: 2; y = y_hi * 2 + y_lo), z: 8, core: 2. Of those that a mesh axis runs over, the one named last changes fastest.
Arguments:
- observations: bfloat16 [81, 4194304], P(None, ('region', 'group')), may hold values from -13 to 13
- obs_index: int32 [16384, 2048], P(('region', 'group')), may hold values from 0 to 8191
- obs_count: int32 [16384], P(('region', 'group')), may hold values from 0 to 2048, as said below
- localization: float32 [16384, 2048], P(('region', 'group')), may hold values from 0.1 to 1
- background: bfloat16 [16384, 80, 512], P(('region', 'group')), may hold values from -6 to 6
- background_mean: float32 [16384, 512], P(('region', 'group')), may hold values from -6 to 6
Outputs:
- analysis: bfloat16 [16384, 80, 512], P(('region', 'group'))
Inputs may be any that keep to these rules, and one draw needn't show every extreme that they name: `obs_count`: A block has either no local observations (count 0) or at least 256 of them; most devices own some blocks without observations, and some device has all its blocks observed.
All inputs are finite; a program needn't handle non-finite values.
Results may differ from a plain program's by a relative error of at most 0.0027.
Values may be sent and summed in bfloat16 or wider, within the bound.
No kernel may reach another device: no remote copies, remote signals or barrier semaphores. Data moves between devices by JAX's collectives and lax.ppermute only.
A program may use at most 32 MiB of HBM per device.

v0:
```python
import math

import jax
import jax.numpy as jnp
from jax import lax
from jax.sharding import PartitionSpec as P

HALO = 2048
NS_ITERS = 6


solve_batch = 4
gram_group = 4


def extended_2(value, sides, width):
    for axis, dim in sides:
        count, length = (lax.axis_size(axis), value.shape[dim])
        up = [(i, (i + 1) % count) for i in range(count)]
        down = [(j, i) for i, j in up]
        last = lax.slice_in_dim(value, length - width, length, axis=dim)
        initial = lax.slice_in_dim(value, 0, width, axis=dim)
        before = lax.ppermute(last, axis, up)
        after = lax.ppermute(initial, axis, down)
        value = jnp.concatenate([before, value, after], axis=dim)
    return value


def matmul_high(left, right):
    return jnp.einsum("nij,njk->nik", left, right, precision=lax.Precision.HIGHEST)


def solve_weights(gram):
    members = gram.shape[1] - 1
    identity = jnp.eye(members, dtype=jnp.float32)
    information = gram[:, :members, :members] + (members - 1.0) * identity
    innovation_term = gram[:, :members, members]
    scale = jnp.sqrt(jnp.sum(information * information, axis=(1, 2)))
    iterate_y = information / scale[:, None, None]
    iterate_z = jnp.broadcast_to(identity, information.shape)
    for sweep in range(NS_ITERS):
        factor = 1.5 * identity - 0.5 * matmul_high(iterate_z, iterate_y)
        iterate_y = matmul_high(iterate_y, factor)
        iterate_z = matmul_high(factor, iterate_z)
    spread_part = math.sqrt(members - 1.0) * iterate_z / jnp.sqrt(scale)[:, None, None]
    covariance = matmul_high(iterate_z, iterate_z) / scale[:, None, None]
    mean_shift = jnp.einsum(
        "nij,nj->ni", covariance, innovation_term, precision=lax.Precision.HIGHEST
    )
    return spread_part + mean_shift[:, :, None]


def solve_active(grams, active):
    total_items = grams.shape[0]
    members = grams.shape[1] - 1
    active_int = active.astype(jnp.int32)
    active_count = jnp.sum(active_int)
    rank_on = jnp.cumsum(active_int) - 1
    rank_off = active_count + jnp.cumsum(1 - active_int) - 1
    position = jnp.where(active, rank_on, rank_off)
    placing = (position[None, :] == jnp.arange(total_items, dtype=jnp.int32)[:, None]).astype(
        jnp.float32
    )
    packed = jnp.einsum("qb,bkl->qkl", placing, grams, precision=lax.Precision.HIGHEST)
    batches = (active_count + solve_batch - 1) // solve_batch

    def one_batch(batch_step, results):
        offset = batch_step * solve_batch
        block_piece = lax.dynamic_slice_in_dim(packed, offset, solve_batch, 0)
        return lax.dynamic_update_slice_in_dim(results, solve_weights(block_piece), offset, 0)

    results = lax.fori_loop(
        0, batches, one_batch, jnp.zeros((total_items, members, members), jnp.float32)
    )
    unpacked = jnp.einsum("qb,qij->bij", placing, results, precision=lax.Precision.HIGHEST)
    identity = jnp.eye(members, dtype=jnp.float32)
    return jnp.where(active[:, None, None], unpacked, identity).astype(jnp.bfloat16)


def on_device(observations, obs_index, obs_count, localization, background, background_mean):
    rows = observations.shape[0]
    total_blocks = obs_index.shape[0]
    p_most = obs_index.shape[1]
    extended = extended_2(observations, (("region", 1),), HALO)
    within = (jnp.arange(p_most, dtype=jnp.int32)[None, :] < obs_count[:, None]).astype(jnp.float32)
    factors = (localization * within).reshape(total_blocks // gram_group, gram_group, p_most)
    index_groups = obs_index.reshape(total_blocks // gram_group, gram_group, p_most)

    def group_gram(pieces):
        index_piece, factor_piece = pieces
        local = jnp.take(extended, index_piece, axis=1)
        weighted = (local * factor_piece[None]).astype(jnp.bfloat16)
        return jnp.einsum("kbp,lbp->bkl", weighted, local, preferred_element_type=jnp.float32)

    gram = lax.map(group_gram, (index_groups, factors)).reshape(total_blocks, rows, rows)
    active = obs_count > 0
    weights = solve_active(gram, active)
    mixed = jnp.einsum("bji,bjr->bir", weights, background, preferred_element_type=jnp.float32)
    return (background_mean[:, None, :] + mixed).astype(jnp.bfloat16)


def solution(mesh):
    return jax.shard_map(
        on_device,
        mesh=mesh,
        in_specs=(
            P(None, ("region", "group")),
            P(("region", "group"), None),
            P(("region", "group")),
            P(("region", "group"), None),
            P(("region", "group"), None, None),
            P(("region", "group"), None),
        ),
        out_specs=P(("region", "group"), None, None),
        check_vma=False,
    )
```

profile of v0, /device:TPU:33, one launch (start us, length us, event | category | flops | bytes accessed | tf_op | source)
XLA Modules:
  0.0 220.5 jit_solution(4182884997619381877)
XLA Ops:
  0.0 1.7 copy.19
  1.7 1.0 fusion.41
  2.7 4.9 %collective-permute-start = (bf16[81,2048]{0,1:T(8,128)(2,1)}, bf16[81,2048]{0,1:T(8,128)(2,1)}, u32[]{:S(2)}, u32[]{:S(2)}) collective-permute-start(bf16[81,2048]{0,1:T(8,128)(2,1)} %get-tuple-element.77), channel_id=1, source_target_pairs={{0,8},{8,16},{16,24},{24,32},{32,40},{40,48},{48,56},{56,64},{64,7... | collective-permute-start | bytes 995336 | tf_op jit(solution)/shard_map/ppermute | solution.py:23
  7.6 17.5 %collective-permute-start.1 = (bf16[81,2048]{0,1:T(8,128)(2,1)S(1)}, bf16[81,2048]{0,1:T(8,128)(2,1)}, u32[]{:S(2)}, u32[]{:S(2)}) collective-permute-start(bf16[81,2048]{0,1:T(8,128)(2,1)S(1)} %get-tuple-element.78), channel_id=1, source_target_pairs={{8,0},{16,8},{24,16},{32,24},{40,32},{48,40},{56,48},{64,56},{72,6... | collective-permute-start | bytes 995336 | tf_op jit(solution)/shard_map/ppermute | solution.py:24
  27.6 0.8 add_reduce_fusion
  29.0 6.1 %collective-permute-done = bf16[81,2048]{0,1:T(8,128)(2,1)} collective-permute-done((bf16[81,2048]{0,1:T(8,128)(2,1)}, bf16[81,2048]{0,1:T(8,128)(2,1)}, u32[]{:S(2)}, u32[]{:S(2)}) %collective-permute-start) | collective-permute-done | bytes 331808 | tf_op jit(solution)/shard_map/ppermute | solution.py:23
  35.7 1.9 pad_maximum_fusion
  37.6 151.7 %while.20 = (s32[]{:T(128)}, f32[4,4,81,81]{3,2,1,0:T(8,128)}, s32[4,4,2048]{2,1,0:T(4,128)S(1)}, bf16[81,8192]{0,1:T(8,128)(2,1)S(1)}, f32[4,4,2048]{2,1,0:T(4,128)}, /*index=5*/s32[]{:T(128)}) while((s32[]{:T(128)}, f32[4,4,81,81]{3,2,1,0:T(8,128)}, s32[4,4,2048]{2,1,0:T(4,128)S(1)}, bf16[81,8192]{0,1:T(8,128)(2,1)S(1)}, ...), condition=%wide.region_4.5_spmd, body=%wide.region_3.4_spmd.sunk | while | flops 110895104 | bytes 9806473 | solution.py:95
  38.3 29.4 %gather_fusion = bf16[8192,81]{1,0:T(8,128)(2,1)} fusion(bf16[81,8192]{0,1:T(8,128)(2,1)S(1)} %get-tuple-element.161, s32[8192]{0:T(1024)S(1)} %broadcast_clamp_fusion.2), kind=kCustom, calls=%fused_computation.clone.1 | custom fusion | bytes 2686976 | tf_op jit(solution)/shard_map/while/body/eval_jaxpr/jit(_take)/gather | solution.py:91
  67.7 3.9 %copy.43 = bf16[4,2048,81]{1,2,0:T(8,128)(2,1)} copy(bf16[4,2048,81]{2,1,0:T(8,128)(2,1)} %bitcast.173) | data formatting | bytes 2654208 | tf_op jit(solution)/shard_map/while/body/eval_jaxpr/jit(_take)/gather | solution.py:91
  71.6 0.8 dynamic-slice_bitcast_fusion.2
  72.3 3.2 %fusion.157 = f32[4,4,81,81]{3,2,1,0:T(8,128)} fusion(f32[4,4,81,81]{3,2,1,0:T(8,128)} %get-tuple-element.153, s32[]{:T(128)} %get-tuple-element.152, bf16[4,2048,81]{1,2,0:T(8,128)(2,1)} %copy.43, pred[4,2048]{1,0:T(4,128)(4,1)S(1)} %compare_and_fusion.2, f32[4,2048]{1,0:T(4,128)S(1)} %dynamic-slice_bitcast_fusion.2), kind=kOutput, calls=%fused_computation.37.clone.1 | convolution fusion | flops 110813184 | bytes 3113472 | tf_op jit(solution)/shard_map/while/body/eval_jaxpr/kbp,lbp->bkl/dot_general | solution.py:93
  76.2 29.4 %gather_fusion = bf16[8192,81]{1,0:T(8,128)(2,1)} fusion(bf16[81,8192]{0,1:T(8,128)(2,1)S(1)} %get-tuple-element.161, s32[8192]{0:T(1024)S(1)} %broadcast_clamp_fusion.2), kind=kCustom, calls=%fused_computation.clone.1 | custom fusion | bytes 2686976 | tf_op jit(solution)/shard_map/while/body/eval_jaxpr/jit(_take)/gather | solution.py:91
  105.6 3.9 %copy.43 = bf16[4,2048,81]{1,2,0:T(8,128)(2,1)} copy(bf16[4,2048,81]{2,1,0:T(8,128)(2,1)} %bitcast.173) | data formatting | bytes 2654208 | tf_op jit(solution)/shard_map/while/body/eval_jaxpr/jit(_take)/gather | solution.py:91
  110.3 3.2 %fusion.157 = f32[4,4,81,81]{3,2,1,0:T(8,128)} fusion(f32[4,4,81,81]{3,2,1,0:T(8,128)} %get-tuple-element.153, s32[]{:T(128)} %get-tuple-element.152, bf16[4,2048,81]{1,2,0:T(8,128)(2,1)} %copy.43, pred[4,2048]{1,0:T(4,128)(4,1)S(1)} %compare_and_fusion.2, f32[4,2048]{1,0:T(4,128)S(1)} %dynamic-slice_bitcast_fusion.2), kind=kOutput, calls=%fused_computation.37.clone.1 | convolution fusion | flops 110813184 | bytes 3113472 | tf_op jit(solution)/shard_map/while/body/eval_jaxpr/kbp,lbp->bkl/dot_general | solution.py:93
  114.1 29.4 %gather_fusion = bf16[8192,81]{1,0:T(8,128)(2,1)} fusion(bf16[81,8192]{0,1:T(8,128)(2,1)S(1)} %get-tuple-element.161, s32[8192]{0:T(1024)S(1)} %broadcast_clamp_fusion.2), kind=kCustom, calls=%fused_computation.clone.1 | custom fusion | bytes 2686976 | tf_op jit(solution)/shard_map/while/body/eval_jaxpr/jit(_take)/gather | solution.py:91
  143.5 3.9 %copy.43 = bf16[4,2048,81]{1,2,0:T(8,128)(2,1)} copy(bf16[4,2048,81]{2,1,0:T(8,128)(2,1)} %bitcast.173) | data formatting | bytes 2654208 | tf_op jit(solution)/shard_map/while/body/eval_jaxpr/jit(_take)/gather | solution.py:91
  148.2 3.2 %fusion.157 = f32[4,4,81,81]{3,2,1,0:T(8,128)} fusion(f32[4,4,81,81]{3,2,1,0:T(8,128)} %get-tuple-element.153, s32[]{:T(128)} %get-tuple-element.152, bf16[4,2048,81]{1,2,0:T(8,128)(2,1)} %copy.43, pred[4,2048]{1,0:T(4,128)(4,1)S(1)} %compare_and_fusion.2, f32[4,2048]{1,0:T(4,128)S(1)} %dynamic-slice_bitcast_fusion.2), kind=kOutput, calls=%fused_computation.37.clone.1 | convolution fusion | flops 110813184 | bytes 3113472 | tf_op jit(solution)/shard_map/while/body/eval_jaxpr/kbp,lbp->bkl/dot_general | solution.py:93
  152.0 29.4 %gather_fusion = bf16[8192,81]{1,0:T(8,128)(2,1)} fusion(bf16[81,8192]{0,1:T(8,128)(2,1)S(1)} %get-tuple-element.161, s32[8192]{0:T(1024)S(1)} %broadcast_clamp_fusion.2), kind=kCustom, calls=%fused_computation.clone.1 | custom fusion | bytes 2686976 | tf_op jit(solution)/shard_map/while/body/eval_jaxpr/jit(_take)/gather | solution.py:91
  181.5 3.9 %copy.43 = bf16[4,2048,81]{1,2,0:T(8,128)(2,1)} copy(bf16[4,2048,81]{2,1,0:T(8,128)(2,1)} %bitcast.173) | data formatting | bytes 2654208 | tf_op jit(solution)/shard_map/while/body/eval_jaxpr/jit(_take)/gather | solution.py:91
  186.1 3.2 %fusion.157 = f32[4,4,81,81]{3,2,1,0:T(8,128)} fusion(f32[4,4,81,81]{3,2,1,0:T(8,128)} %get-tuple-element.153, s32[]{:T(128)} %get-tuple-element.152, bf16[4,2048,81]{1,2,0:T(8,128)(2,1)} %copy.43, pred[4,2048]{1,0:T(4,128)(4,1)S(1)} %compare_and_fusion.2, f32[4,2048]{1,0:T(4,128)S(1)} %dynamic-slice_bitcast_fusion.2), kind=kOutput, calls=%fused_computation.37.clone.1 | convolution fusion | flops 110813184 | bytes 3113472 | tf_op jit(solution)/shard_map/while/body/eval_jaxpr/kbp,lbp->bkl/dot_general | solution.py:93
  189.3 1.5 copy.26
  191.3 26.7 %while.21 = (s32[]{:T(128)}, f32[16,80,80]{2,0,1:T(8,128)S(1)}, s32[]{:T(128)}, f32[16,81,81]{1,0,2:T(8,128)S(1)}, s32[]{:T(128)}, /*index=5*/s32[]{:T(128)}, s32[]{:T(128)}, s32[]{:T(128)}, s32[]{}) while((s32[]{:T(128)}, f32[16,80,80]{2,0,1:T(8,128)S(1)}, s32[]{:T(128)}, f32[16,81,81]{1,0,2:T(8,128)S(1)}, s32[]{:T(128)}, ...), condition=%wide.region_7.8_spmd, body=%wide.region_5.7_spmd.sunk | while | flops 443251200 | bytes 7169563 | solution.py:72
  218.9 1.6 add_convert_fusion
  (194 shorter events, 35.0 us)
Async XLA Ops:
  0.0 218.9 %copy-start = (bf16[16,80,512]{2,1,0:T(8,128)(2,1)S(1)}, bf16[16,80,512]{2,1,0:T(8,128)(2,1)}, u32[]{:S(2)}) copy-start(bf16[16,80,512]{2,1,0:T(8,128)(2,1)} %param.14) | copy-start | bytes 3932164
  0.0 25.1 %copy-start.8 = (s32[16]{0:T(128)S(1)}, s32[16]{0:T(128)}, u32[]{:S(2)}) copy-start(s32[16]{0:T(128)} %param.12) | copy-start | bytes 196
  0.0 26.8 %copy-start.4 = (f32[16,2048]{1,0:T(8,128)S(1)}, f32[16,2048]{1,0:T(8,128)}, u32[]{:S(2)}) copy-start(f32[16,2048]{1,0:T(8,128)} %param.13) | copy-start | bytes 393220
  0.0 27.6 %copy-start.5 = (s32[16,2048]{1,0:T(8,128)S(1)}, s32[16,2048]{1,0:T(8,128)}, u32[]{:S(2)}) copy-start(s32[16,2048]{1,0:T(8,128)} %param.11) | copy-start | bytes 393220
  1.7 33.4 %copy-start.1 = (bf16[81,4096]{0,1:T(8,128)(2,1)}, bf16[81,4096]{0,1:T(8,128)(2,1)S(1)}, u32[]{:S(2)}) copy-start(bf16[81,4096]{0,1:T(8,128)(2,1)S(1)} %copy.19) | copy-start | bytes 1990660
  2.7 32.4 %collective-permute-start = (bf16[81,2048]{0,1:T(8,128)(2,1)}, bf16[81,2048]{0,1:T(8,128)(2,1)}, u32[]{:S(2)}, u32[]{:S(2)}) collective-permute-start(bf16[81,2048]{0,1:T(8,128)(2,1)} %get-tuple-element.77), channel_id=1, source_target_pairs={{0,8},{8,16},{16,24},{24,32},{32,40},{40,48},{48,56},{56,64},{64,7... | collective-permute-start | bytes 995336 | tf_op jit(solution)/shard_map/ppermute | solution.py:23
  7.6 28.1 %collective-permute-start.1 = (bf16[81,2048]{0,1:T(8,128)(2,1)S(1)}, bf16[81,2048]{0,1:T(8,128)(2,1)}, u32[]{:S(2)}, u32[]{:S(2)}) collective-permute-start(bf16[81,2048]{0,1:T(8,128)(2,1)S(1)} %get-tuple-element.78), channel_id=1, source_target_pairs={{8,0},{16,8},{24,16},{32,24},{40,32},{48,40},{56,48},{64,56},{72,6... | collective-permute-start | bytes 995336 | tf_op jit(solution)/shard_map/ppermute | solution.py:24
  37.6 0.7 copy-start.2
  67.7 3.9 %copy-start.3 = (s32[4,4,2048]{2,1,0:T(4,128)S(1)}, s32[4,4,2048]{2,1,0:T(4,128)}, u32[]{:S(2)}) copy-start(s32[4,4,2048]{2,1,0:T(4,128)} %copy-done.2) | copy-start | bytes 393220 | tf_op jit(solution)/shard_map/while
  75.5 0.7 copy-start.2
  105.6 3.9 %copy-start.3 = (s32[4,4,2048]{2,1,0:T(4,128)S(1)}, s32[4,4,2048]{2,1,0:T(4,128)}, u32[]{:S(2)}) copy-start(s32[4,4,2048]{2,1,0:T(4,128)} %copy-done.2) | copy-start | bytes 393220 | tf_op jit(solution)/shard_map/while
  113.4 0.7 copy-start.2
  143.5 3.9 %copy-start.3 = (s32[4,4,2048]{2,1,0:T(4,128)S(1)}, s32[4,4,2048]{2,1,0:T(4,128)}, u32[]{:S(2)}) copy-start(s32[4,4,2048]{2,1,0:T(4,128)} %copy-done.2) | copy-start | bytes 393220 | tf_op jit(solution)/shard_map/while
  151.4 0.7 copy-start.2
  181.5 3.9 %copy-start.3 = (s32[4,4,2048]{2,1,0:T(4,128)S(1)}, s32[4,4,2048]{2,1,0:T(4,128)}, u32[]{:S(2)}) copy-start(s32[4,4,2048]{2,1,0:T(4,128)} %copy-done.2) | copy-start | bytes 393220 | tf_op jit(solution)/shard_map/while
  191.3 27.6 %copy-start.6 = (bf16[80,80]{0,1:T(8,128)(2,1)S(1)}, bf16[80,80]{0,1:T(8,128)(2,1)}, u32[]{:S(2)}) copy-start(bf16[80,80]{0,1:T(8,128)(2,1)} %fusion.32) | copy-start | bytes 38404
  191.3 27.6 %copy-start.7 = (f32[16,512]{1,0:T(8,128)S(1)}, f32[16,512]{1,0:T(8,128)}, u32[]{:S(2)}) copy-start(f32[16,512]{1,0:T(8,128)} %param.15) | copy-start | bytes 98308
where the time goes:
time: 221 us
  local copies, waits for them, and re-layouts  146 us (66%)
  matrix products  37 us (17%)
  starting transfers between devices  22.4 us (10%)
  other arithmetic  6.63 us (3%)
  waiting for transfers between devices  6.61 us (3%)
    gather x8, local copies, waits for them, and re-layouts, group_gram(): local = jnp.take(extended, index_piece, axis=1)  133 us
    dot_general x72, matrix products, matmul_high(): jnp.einsum('nij,njk->nik', left, right, precision=lax.Precision.HIGHEST)  20.8 us
    ppermute x1, starting transfers between devices, extended_2(): after = lax.ppermute(initial, axis, down)  17.5 us
    dot_general x4, matrix products, group_gram(): jnp.einsum('kbp,lbp->bkl', weighted, local, preferred_element_type=jnp.fl...  12.7 us
    ppermute x1, waiting for transfers between devices, extended_2(): before = lax.ppermute(last, axis, up)  6.06 us
    ppermute x1, starting transfers between devices, extended_2(): before = lax.ppermute(last, axis, up)  4.9 us
  transfers between devices with their start and end apart: 2, of which 2 were waited for; matrix products, arithmetic and copies ran while one was open for 1% of the time, Pallas kernels for 0%

commit v1 on v0

v1 whole, which is shorter than its diff:
```python
import functools
import math

import jax
import jax.numpy as jnp
from jax import lax
from jax.experimental import pallas as pl
from jax.experimental.pallas import tpu as pltpu
from jax.sharding import PartitionSpec as P

HALO = 2048
NS_ITERS = 6
LANES = 128
BF16 = jnp.bfloat16
F32 = jnp.float32
NT = (((1,), (1,)), ((), ()))

hist_unroll = 2
gram_chunk = 8
solve_batch = 4


def histogram(block, count_ref, index_ref, factor_ref, w_ref):
    blocks, p_most = index_ref.shape
    groups = w_ref.shape[0] // blocks
    index = index_ref[pl.ds(block, 1), :]
    factor = factor_ref[pl.ds(block, 1), :]
    place = lax.broadcasted_iota(jnp.int32, (1, p_most), 1)
    factor = jnp.where(place < count_ref[block], factor, 0.0)
    hi = lax.shift_right_logical(index, 7)
    lo = lax.bitwise_and(index, LANES - 1)
    hi_at = lax.broadcasted_iota(jnp.int32, (groups, p_most), 0)
    lo_at = lax.broadcasted_iota(jnp.int32, (LANES, p_most), 0)
    hi_hot = jnp.where(hi_at == hi, factor, 0.0).astype(BF16)
    lo_hot = jnp.where(lo_at == lo, 1.0, 0.0).astype(BF16)
    summed = lax.dot_general(hi_hot, lo_hot, NT, preferred_element_type=F32)
    w_ref[pl.ds(block, groups, stride=blocks), :] = summed


def gram_part(record, w_ref, first, blocks):
    members = record.shape[0] - 1
    pieces = []
    for j in range(record.shape[1] // LANES):
        columns = slice(j * LANES, (j + 1) * LANES)
        perturbations = record[:members, columns]
        innovation = record[members:, columns].astype(F32)
        w = w_ref[pl.ds(pl.multiple_of((first + j) * blocks, blocks), blocks), :]
        rows = []
        for b in range(blocks):
            w_b = jnp.broadcast_to(w[b : b + 1, :], (16, LANES)).astype(BF16)
            rows.append(perturbations * jnp.concatenate([w_b] * (members // 16), axis=0))
        rows.append(w.astype(BF16) * jnp.broadcast_to(innovation, (blocks, LANES)).astype(BF16))
        pieces.append(jnp.concatenate(rows, axis=0))
    weighted = jnp.concatenate(pieces, axis=1)
    return lax.dot_general(weighted, record[:members], NT, preferred_element_type=F32)


def add_gram(record_ref, w_ref, first, blocks, sum_ref):
    width = gram_chunk * LANES

    def step(c, carry):
        record = record_ref[:, pl.ds(pl.multiple_of(c * width, width), width)]
        sum_ref[...] += gram_part(record, w_ref, first + c * gram_chunk, blocks)
        return carry

    lax.fori_loop(0, record_ref.shape[1] // width, step, 0)


def own_gram_kernel(count_ref, index_ref, factor_ref, record_ref, gram_ref, w_ref):
    blocks = index_ref.shape[0]

    def step(i, carry):
        for j in range(hist_unroll):
            histogram(i * hist_unroll + j, count_ref, index_ref, factor_ref, w_ref)
        return carry

    lax.fori_loop(0, blocks // hist_unroll, step, 0)
    gram_ref[...] = jnp.zeros_like(gram_ref)
    add_gram(record_ref, w_ref, HALO // LANES, blocks, gram_ref)


def own_gram(obs_count, obs_index, localization, record):
    blocks, p_most = obs_index.shape
    rows, columns = record.shape
    groups = (columns + 2 * HALO) // LANES
    vmem = pl.BlockSpec(memory_space=pltpu.VMEM)
    return pl.pallas_call(
        own_gram_kernel,
        out_shape=(
            jax.ShapeDtypeStruct((blocks * rows, rows - 1), F32),
            jax.ShapeDtypeStruct((groups * blocks, LANES), F32),
        ),
        in_specs=[pl.BlockSpec(memory_space=pltpu.SMEM), vmem, vmem, vmem],
        out_specs=(vmem, vmem),
        compiler_params=pltpu.CompilerParams(vmem_limit_bytes=40 * 2**20),
        cost_estimate=pl.CostEstimate(
            flops=8_000_000_000, bytes_accessed=8_000_000, transcendentals=0
        ),
        name="own_gram",
    )(obs_count, obs_index, localization, record)


def three(x):
    return jnp.concatenate([x, x, x], axis=1)


def left_terms(x):
    third = x.shape[1] // 3
    lane = lax.broadcasted_iota(jnp.int32, x.shape, 1)
    middle = (lane >= third) & (lane < 2 * third)
    return jnp.where(middle, x - x.astype(BF16).astype(F32), x).astype(BF16)


def right_terms(x):
    upper = x.astype(BF16)
    lower = (x - upper.astype(F32)).astype(BF16)
    return jnp.concatenate([upper, upper, lower], axis=0)


def solve_blocks(informations, innovations):
    members = informations[0].shape[0]
    row_at = lax.broadcasted_iota(jnp.int32, (members, members), 0)
    column_at = lax.broadcasted_iota(jnp.int32, (members, members), 1)
    eye = (row_at == column_at).astype(F32)
    eye_3 = three(eye)
    s, z, t, squares = [], [], [], []
    for gram, innovation in zip(informations, innovations):
        information = gram + (members - 1.0) * eye
        square = jnp.sum(information * information, axis=1, keepdims=True)
        square = jnp.sum(square, axis=0, keepdims=True)
        squares.append(square)
        s.append(three(information * lax.rsqrt(square)))
        t.append(jnp.broadcast_to(three(innovation), (8, 3 * members)))
        z.append(None)
    for sweep in range(NS_ITERS):
        final = sweep == NS_ITERS - 1
        rights = [right_terms(x) for x in s]
        for i in range(len(s)):
            lefts = ([] if final else [s[i]]) + ([z[i]] if sweep else []) + [t[i]]
            product = jnp.dot(
                left_terms(jnp.concatenate(lefts, axis=0)), rights[i], preferred_element_type=F32
            )
            at = 0 if final else members
            if sweep:
                z[i] = 1.5 * z[i] - 0.5 * product[at : at + members]
            else:
                z[i] = 1.5 * eye_3 - 0.5 * s[i]
            if not final:
                s[i] = 1.5 * s[i] - 0.5 * product[:members]
            t[i] = 1.5 * t[i] - 0.5 * product[-8:]
        for i in range(len(s)):
            lefts = ([] if final else [s[i]]) + [t[i]]
            product = jnp.dot(
                left_terms(jnp.concatenate(lefts, axis=0)), rights[i], preferred_element_type=F32
            )
            if not final:
                s[i] = 1.5 * s[i] - 0.5 * product[:members]
            t[i] = 1.5 * t[i] - 0.5 * product[-8:]
    solved = []
    for square, z_i, t_i in zip(squares, z, t):
        inverse = lax.rsqrt(square)
        spread = (math.sqrt(members - 1.0) * jnp.sqrt(inverse)) * z_i[:, :members]
        solved.append(spread + inverse * t_i[:1, :members])
    return solved, eye


def finish_kernel(
    count_ref, own_ref, w_ref, lower_ref, upper_ref, background_ref, mean_ref, out_ref, gram_ref
):
    step = pl.program_id(0)
    blocks = count_ref.shape[0]
    members = background_ref.shape[1]

    @pl.when(step == 0)
    def _():
        gram_ref[...] = own_ref[...]
        groups = w_ref.shape[0] // blocks
        add_gram(lower_ref, w_ref, 0, blocks, gram_ref)
        add_gram(upper_ref, w_ref, groups - HALO // LANES, blocks, gram_ref)

    informations, innovations = [], []
    for i in range(solve_batch):
        b = step * solve_batch + i
        informations.append(gram_ref[pl.ds(pl.multiple_of(b * members, members), members), :])
        innovations.append(gram_ref[pl.ds(blocks * members + b, 1), :])
    solved, eye = solve_blocks(informations, innovations)
    for i in range(solve_batch):
        b = step * solve_batch + i
        weights = jnp.where(count_ref[b] > 0, solved[i], eye).astype(BF16)
        mixed = jnp.dot(weights, background_ref[i], preferred_element_type=F32)
        out_ref[i] = (mean_ref[pl.ds(b, 1), :] + mixed).astype(BF16)


def finish(obs_count, own, w, lower, upper, background, background_mean):
    blocks, members, cells = background.shape

    def whole(x):
        return pl.BlockSpec(x.shape, lambda i: (0,) * x.ndim)

    states = pl.BlockSpec((solve_batch, members, cells), lambda i: (i, 0, 0))
    return pl.pallas_call(
        finish_kernel,
        grid=(blocks // solve_batch,),
        out_shape=jax.ShapeDtypeStruct(background.shape, BF16),
        in_specs=[
            pl.BlockSpec(memory_space=pltpu.SMEM),
            whole(own),
            whole(w),
            whole(lower),
            whole(upper),
            states,
            whole(background_mean),
        ],
        out_specs=states,
        scratch_shapes=[pltpu.VMEM(own.shape, F32)],
        compiler_params=pltpu.CompilerParams(vmem_limit_bytes=40 * 2**20),
        name="finish",
    )(obs_count, own, w, lower, upper, background, background_mean)


def on_device(observations, obs_index, obs_count, localization, background, background_mean):
    count = lax.axis_size("region")
    up = [(i, (i + 1) % count) for i in range(count)]
    down = [(j, i) for i, j in up]
    own_columns = observations.shape[1]
    lower = lax.ppermute(observations[:, own_columns - HALO :], "region", up)
    upper = lax.ppermute(observations[:, :HALO], "region", down)
    own, w = own_gram(obs_count, obs_index, localization, observations)
    return finish(obs_count, own, w, lower, upper, background, background_mean)


def solution(mesh):
    return jax.shard_map(
        on_device,
        mesh=mesh,
        in_specs=(
            P(None, ("region", "group")),
            P(("region", "group"), None),
            P(("region", "group")),
            P(("region", "group"), None),
            P(("region", "group"), None, None),
            P(("region", "group"), None),
        ),
        out_specs=P(("region", "group"), None, None),
        check_vma=False,
    )
```

time: 221 us -> 52.3 us (0.24)
  the two profiles are of different devices: /device:TPU:33 before, /device:TPU:1 now
where the time goes in v1:
time: 52.3 us; the launch traced here: 51.8 us
  starting transfers between devices  23.4 us (45%)
  Pallas kernels  22 us (42%)
  waiting for transfers between devices  5.1 us (10%)
  local copies, waits for them, and re-layouts  1.25 us (2%)
    ppermute x1, starting transfers between devices, on_device(): upper = lax.ppermute(observations[:, :HALO], 'region', down)  21.3 us
    pallas_call x1, Pallas kernels, finish(): pl.pallas_call(finish_kernel, grid=(blocks // solve_batch,), out_shape=ja...  14 us
    pallas_call x1, Pallas kernels, own_gram(): pl.pallas_call(own_gram_kernel, out_shape=(jax.ShapeDtypeStruct((blocks *...  8 us
    ppermute x1, waiting for transfers between devices, on_device(): lower = lax.ppermute(observations[:, own_columns - HALO:], 'region', up)  5.09 us
    ppermute x1, starting transfers between devices, on_device(): lower = lax.ppermute(observations[:, own_columns - HALO:], 'region', up)  2.05 us
    slice x1, local copies, waits for them, and re-layouts, on_device(): upper = lax.ppermute(observations[:, :HALO], 'region', down)  1.22 us
  transfers between devices with their start and end apart: 2, of which 1 were waited for; matrix products, arithmetic and copies ran while one was open for 0% of the time, Pallas kernels for 15%

profile of v1, /device:TPU:1, one launch (start us, length us, event | category | flops | bytes accessed | tf_op | source)
XLA Modules:
  0.0 51.8 jit_solution(10574785433546618034)
XLA Ops:
  0.0 0.0 copy-start.1
  0.0 0.0 copy-start.3
  0.0 0.0 copy-start.5
  0.0 0.0 copy-start.4
  0.0 1.2 %fusion = (bf16[81,2048]{1,0:T(8,128)(2,1)S(1)}, bf16[81,2048]{1,0:T(8,128)(2,1)S(1)}) fusion(bf16[81,4096]{1,0:T(8,128)(2,1)} %record_ref.1), kind=kLoop, calls=%fused_computation | loop fusion | bytes 1327104 | tf_op jit(solution)/shard_map/slice | solution.py:227
  1.3 21.3 %collective-permute-start.1 = (bf16[81,2048]{1,0:T(8,128)(2,1)S(1)}, bf16[81,2048]{1,0:T(8,128)(2,1)S(1)}, u32[]{:S(2)}, u32[]{:S(2)}) collective-permute-start(bf16[81,2048]{1,0:T(8,128)(2,1)S(1)} %get-tuple-element.9), channel_id=1, source_target_pairs={{8,0},{16,8},{24,16},{32,24},{40,32},{48,40},{56,48},{64,56},{72,6... | collective-permute-start | bytes 995336 | tf_op jit(solution)/shard_map/ppermute | solution.py:227
  22.6 0.0 copy-start
  22.6 0.0 copy-start.2
  22.6 2.1 %collective-permute-start = (bf16[81,2048]{1,0:T(8,128)(2,1)S(1)}, bf16[81,2048]{1,0:T(8,128)(2,1)S(1)}, u32[]{:S(2)}, u32[]{:S(2)}) collective-permute-start(bf16[81,2048]{1,0:T(8,128)(2,1)S(1)} %get-tuple-element.10), channel_id=1, source_target_pairs={{0,8},{8,16},{16,24},{24,32},{32,40},{40,48},{48,56},{56,64},{64,7... | collective-permute-start | bytes 995336 | tf_op jit(solution)/shard_map/ppermute | solution.py:226
  24.6 0.0 copy-done.1
  24.7 0.0 copy-done.3
  24.7 0.0 copy-done.5
  24.7 0.0 copy-done.4
  24.7 8.0 %own_gram.1 = (f32[1296,80]{1,0:T(8,128)S(1)}, f32[1024,128]{1,0:T(8,128)S(1)}) custom-call(s32[16]{0:T(128)S(1)} %copy-done.3, s32[16,2048]{1,0:T(8,128)S(1)} %copy-done.4, f32[16,2048]{1,0:T(8,128)S(1)} %copy-done.5, bf16[81,4096]{1,0:T(8,128)(2,1)S(1)} %copy-done.1), custom_call_target="tpu_custom_call" | custom-call | flops 8000000000 | bytes 8000000 | tf_op jit(solution)/shard_map/own_gram/pallas_call | solution.py:87
  32.7 0.0 collective-permute-done.1.upper_ref
  32.7 5.1 %collective-permute-done.lower_ref = bf16[81,2048]{1,0:T(8,128)(2,1)S(1)} collective-permute-done((bf16[81,2048]{1,0:T(8,128)(2,1)S(1)}, bf16[81,2048]{1,0:T(8,128)(2,1)S(1)}, u32[]{:S(2)}, u32[]{:S(2)}) %collective-permute-start) | collective-permute-done | bytes 331808 | tf_op jit(solution)/shard_map/ppermute | solution.py:226
  37.8 0.0 copy-done
  37.8 0.0 copy-done.2
  37.8 14.0 %finish.1 = bf16[16,80,512]{2,1,0:T(8,128)(2,1)} custom-call(s32[16]{0:T(128)S(1)} %copy-done.3, f32[1296,80]{1,0:T(8,128)S(1)} %get-tuple-element.7.own_ref, f32[1024,128]{1,0:T(8,128)S(1)} %get-tuple-element.8.w_ref, bf16[81,2048]{1,0:T(8,128)(2,1)S(1)} %collective-permute-done.lower_ref, bf16[81,2048]{1,0:T(8,128)(2,1)S(1)} %collective-permute-done.1.upper_ref, ...), custom_call_target="tpu_custom_call" | custom-call | tf_op jit(solution)/shard_map/finish/pallas_call | solution.py:201
Async XLA Ops:
  0.0 24.6 %copy-start.1 = (bf16[81,4096]{1,0:T(8,128)(2,1)S(1)}, bf16[81,4096]{1,0:T(8,128)(2,1)}, u32[]{:S(2)}) copy-start(bf16[81,4096]{1,0:T(8,128)(2,1)} %record_ref.1) | copy-start | bytes 1990660
  0.0 24.7 %copy-start.3 = (s32[16]{0:T(128)S(1)}, s32[16]{0:T(128)}, u32[]{:S(2)}) copy-start(s32[16]{0:T(128)} %count_ref.3) | copy-start | bytes 196
  0.0 24.7 %copy-start.5 = (f32[16,2048]{1,0:T(8,128)S(1)}, f32[16,2048]{1,0:T(8,128)}, u32[]{:S(2)}) copy-start(f32[16,2048]{1,0:T(8,128)} %factor_ref.1) | copy-start | bytes 393220
  0.0 24.7 %copy-start.4 = (s32[16,2048]{1,0:T(8,128)S(1)}, s32[16,2048]{1,0:T(8,128)}, u32[]{:S(2)}) copy-start(s32[16,2048]{1,0:T(8,128)} %index_ref.1) | copy-start | bytes 393220
  1.3 31.4 %collective-permute-start.1 = (bf16[81,2048]{1,0:T(8,128)(2,1)S(1)}, bf16[81,2048]{1,0:T(8,128)(2,1)S(1)}, u32[]{:S(2)}, u32[]{:S(2)}) collective-permute-start(bf16[81,2048]{1,0:T(8,128)(2,1)S(1)} %get-tuple-element.9), channel_id=1, source_target_pairs={{8,0},{16,8},{24,16},{32,24},{40,32},{48,40},{56,48},{64,56},{72,6... | collective-permute-start | bytes 995336 | tf_op jit(solution)/shard_map/ppermute | solution.py:227
  22.6 15.2 %copy-start = (bf16[16,80,512]{2,1,0:T(8,128)(2,1)S(1)}, bf16[16,80,512]{2,1,0:T(8,128)(2,1)}, u32[]{:S(2)}) copy-start(bf16[16,80,512]{2,1,0:T(8,128)(2,1)} %background_ref.1) | copy-start | bytes 3932164
  22.6 15.2 %copy-start.2 = (f32[16,512]{1,0:T(8,128)S(1)}, f32[16,512]{1,0:T(8,128)}, u32[]{:S(2)}) copy-start(f32[16,512]{1,0:T(8,128)} %mean_ref.1) | copy-start | bytes 98308
  22.6 15.2 %collective-permute-start = (bf16[81,2048]{1,0:T(8,128)(2,1)S(1)}, bf16[81,2048]{1,0:T(8,128)(2,1)S(1)}, u32[]{:S(2)}, u32[]{:S(2)}) collective-permute-start(bf16[81,2048]{1,0:T(8,128)(2,1)S(1)} %get-tuple-element.10), channel_id=1, source_target_pairs={{0,8},{8,16},{16,24},{24,32},{32,40},{40,48},{48,56},{56,64},{64,7... | collective-permute-start | bytes 995336 | tf_op jit(solution)/shard_map/ppermute | solution.py:226

commit v2 on v1

--- a/solution.py
+++ b/solution.py
@@ -10,6 +10,7 @@
 
 HALO = 2048
 NS_ITERS = 6
+RUN = 8
 LANES = 128
 BF16 = jnp.bfloat16
 F32 = jnp.float32
@@ -17,7 +18,7 @@
 
 hist_unroll = 2
 gram_chunk = 8
-solve_batch = 4
+solve_batch = 8
 
 
 def histogram(block, count_ref, index_ref, factor_ref, w_ref):
@@ -66,7 +67,7 @@
     lax.fori_loop(0, record_ref.shape[1] // width, step, 0)
 
 
-def own_gram_kernel(count_ref, index_ref, factor_ref, record_ref, gram_ref, w_ref):
+def own_gram_body(count_ref, index_ref, factor_ref, record_ref, gram_ref, w_ref):
     blocks = index_ref.shape[0]
 
     def step(i, carry):
@@ -79,80 +80,122 @@
     add_gram(record_ref, w_ref, HALO // LANES, blocks, gram_ref)
 
 
-def own_gram(obs_count, obs_index, localization, record):
+def first_turn_kernel(turn_ref, *refs):
+    @pl.when(turn_ref[0] == 0)
+    def _():
+        own_gram_body(*refs)
+
+
+def second_turn_kernel(turn_ref, count, index, factor, record, gram_in, w_in, gram_ref, w_ref):
+    del gram_in, w_in
+
+    @pl.when(turn_ref[0] != 0)
+    def _():
+        own_gram_body(count, index, factor, record, gram_ref, w_ref)
+
+
+def own_gram(turn, obs_count, obs_index, localization, record, made=()):
     blocks, p_most = obs_index.shape
     rows, columns = record.shape
     groups = (columns + 2 * HALO) // LANES
+    smem = pl.BlockSpec(memory_space=pltpu.SMEM)
     vmem = pl.BlockSpec(memory_space=pltpu.VMEM)
     return pl.pallas_call(
-        own_gram_kernel,
+        second_turn_kernel if made else first_turn_kernel,
         out_shape=(
             jax.ShapeDtypeStruct((blocks * rows, rows - 1), F32),
             jax.ShapeDtypeStruct((groups * blocks, LANES), F32),
         ),
-        in_specs=[pl.BlockSpec(memory_space=pltpu.SMEM), vmem, vmem, vmem],
+        in_specs=[smem, smem, vmem, vmem, vmem] + [vmem] * len(made),
         out_specs=(vmem, vmem),
+        input_output_aliases={5: 0, 6: 1} if made else {},
         compiler_params=pltpu.CompilerParams(vmem_limit_bytes=40 * 2**20),
         cost_estimate=pl.CostEstimate(
             flops=8_000_000_000, bytes_accessed=8_000_000, transcendentals=0
         ),
-        name="own_gram",
-    )(obs_count, obs_index, localization, record)
-
-
-def three(x):
-    return jnp.concatenate([x, x, x], axis=1)
-
-
-def left_terms(x):
-    third = x.shape[1] // 3
-    lane = lax.broadcasted_iota(jnp.int32, x.shape, 1)
-    middle = (lane >= third) & (lane < 2 * third)
-    return jnp.where(middle, x - x.astype(BF16).astype(F32), x).astype(BF16)
+        name="own_gram_second" if made else "own_gram_first",
+    )(turn, obs_count, obs_index, localization, record, *made)
+
+
+def upper_gram_kernel(gram_in, w_ref, upper_ref, gram_ref):
+    blocks = gram_in.shape[0] // upper_ref.shape[0]
+    groups = w_ref.shape[0] // blocks
+    gram_ref[...] = gram_in[...]
+    add_gram(upper_ref, w_ref, groups - HALO // LANES, blocks, gram_ref)
+
+
+def upper_gram(own, w, upper):
+    vmem = pl.BlockSpec(memory_space=pltpu.VMEM)
+    return pl.pallas_call(
+        upper_gram_kernel,
+        out_shape=jax.ShapeDtypeStruct(own.shape, F32),
+        in_specs=[vmem, vmem, vmem],
+        out_specs=vmem,
+        input_output_aliases={0: 0},
+        compiler_params=pltpu.CompilerParams(vmem_limit_bytes=40 * 2**20),
+        cost_estimate=pl.CostEstimate(
+            flops=2_000_000_000, bytes_accessed=2_000_000, transcendentals=0
+        ),
+        name="upper_gram",
+    )(own, w, upper)
+
+
+def padded(x):
+    return jnp.concatenate([x, jnp.zeros((x.shape[0], LANES - x.shape[1]), x.dtype)], axis=1)
+
+
+def terms(x):
+    upper = x.astype(BF16)
+    return upper, (x - upper.astype(F32)).astype(BF16)
 
 
 def right_terms(x):
-    upper = x.astype(BF16)
-    lower = (x - upper.astype(F32)).astype(BF16)
-    return jnp.concatenate([upper, upper, lower], axis=0)
+    upper, lower = terms(x)
+    rest = jnp.zeros((LANES - x.shape[0], LANES), BF16)
+    return (
+        jnp.concatenate([upper, rest, upper, rest], axis=0),
+        jnp.concatenate([lower, rest], axis=0),
+    )
+
+
+def multiply(x, right):
+    upper, lower = terms(x)
+    return jnp.dot(
+        jnp.concatenate([upper, lower], axis=1), right[0], preferred_element_type=F32
+    ) + jnp.dot(upper, right[1], preferred_element_type=F32)
 
 
 def solve_blocks(informations, innovations):
     members = informations[0].shape[0]
-    row_at = lax.broadcasted_iota(jnp.int32, (members, members), 0)
-    column_at = lax.broadcasted_iota(jnp.int32, (members, members), 1)
+    row_at = lax.broadcasted_iota(jnp.int32, (members, LANES), 0)
+    column_at = lax.broadcasted_iota(jnp.int32, (members, LANES), 1)
     eye = (row_at == column_at).astype(F32)
-    eye_3 = three(eye)
     s, z, t, squares = [], [], [], []
     for gram, innovation in zip(informations, innovations):
-        information = gram + (members - 1.0) * eye
+        information = padded(gram) + (members - 1.0) * eye
         square = jnp.sum(information * information, axis=1, keepdims=True)
         square = jnp.sum(square, axis=0, keepdims=True)
         squares.append(square)
-        s.append(three(information * lax.rsqrt(square)))
-        t.append(jnp.broadcast_to(three(innovation), (8, 3 * members)))
+        s.append(information * lax.rsqrt(square))
+        t.append(jnp.broadcast_to(padded(innovation), (8, LANES)))
         z.append(None)
     for sweep in range(NS_ITERS):
         final = sweep == NS_ITERS - 1
         rights = [right_terms(x) for x in s]
         for i in range(len(s)):
             lefts = ([] if final else [s[i]]) + ([z[i]] if sweep else []) + [t[i]]
-            product = jnp.dot(
-                left_terms(jnp.concatenate(lefts, axis=0)), rights[i], preferred_element_type=F32
-            )
+            product = multiply(jnp.concatenate(lefts, axis=0), rights[i])
             at = 0 if final else members
             if sweep:
                 z[i] = 1.5 * z[i] - 0.5 * product[at : at + members]
             else:
-                z[i] = 1.5 * eye_3 - 0.5 * s[i]
+                z[i] = 1.5 * eye - 0.5 * s[i]
             if not final:
                 s[i] = 1.5 * s[i] - 0.5 * product[:members]
             t[i] = 1.5 * t[i] - 0.5 * product[-8:]
         for i in range(len(s)):
             lefts = ([] if final else [s[i]]) + [t[i]]
-            product = jnp.dot(
-                left_terms(jnp.concatenate(lefts, axis=0)), rights[i], preferred_element_type=F32
-            )
+            product = multiply(jnp.concatenate(lefts, axis=0), rights[i])
             if not final:
                 s[i] = 1.5 * s[i] - 0.5 * product[:members]
             t[i] = 1.5 * t[i] - 0.5 * product[-8:]
@@ -161,11 +204,11 @@
         inverse = lax.rsqrt(square)
         spread = (math.sqrt(members - 1.0) * jnp.sqrt(inverse)) * z_i[:, :members]
         solved.append(spread + inverse * t_i[:1, :members])
-    return solved, eye
+    return solved, eye[:, :members]
 
 
 def finish_kernel(
-    count_ref, own_ref, w_ref, lower_ref, upper_ref, background_ref, mean_ref, out_ref, gram_ref
+    count_ref, own_ref, w_ref, lower_ref, background_ref, mean_ref, out_ref, gram_ref
 ):
     step = pl.program_id(0)
     blocks = count_ref.shape[0]
@@ -174,9 +217,7 @@
     @pl.when(step == 0)
     def _():
         gram_ref[...] = own_ref[...]
-        groups = w_ref.shape[0] // blocks
         add_gram(lower_ref, w_ref, 0, blocks, gram_ref)
-        add_gram(upper_ref, w_ref, groups - HALO // LANES, blocks, gram_ref)
 
     informations, innovations = [], []
     for i in range(solve_batch):
@@ -191,7 +232,7 @@
         out_ref[i] = (mean_ref[pl.ds(b, 1), :] + mixed).astype(BF16)
 
 
-def finish(obs_count, own, w, lower, upper, background, background_mean):
+def finish(obs_count, own, w, lower, background, background_mean):
     blocks, members, cells = background.shape
 
     def whole(x):
@@ -207,7 +248,6 @@
             whole(own),
             whole(w),
             whole(lower),
-            whole(upper),
             states,
             whole(background_mean),
         ],
@@ -215,7 +255,7 @@
         scratch_shapes=[pltpu.VMEM(own.shape, F32)],
         compiler_params=pltpu.CompilerParams(vmem_limit_bytes=40 * 2**20),
         name="finish",
-    )(obs_count, own, w, lower, upper, background, background_mean)
+    )(obs_count, own, w, lower, background, background_mean)
 
 
 def on_device(observations, obs_index, obs_count, localization, background, background_mean):
@@ -223,10 +263,16 @@
     up = [(i, (i + 1) % count) for i in range(count)]
     down = [(j, i) for i, j in up]
     own_columns = observations.shape[1]
+    place = lax.axis_index("region")
+    turn = jnp.minimum(place % RUN, 1).astype(jnp.int32)[None]
+    given = (turn, obs_count, obs_index, localization, observations)
     lower = lax.ppermute(observations[:, own_columns - HALO :], "region", up)
-    upper = lax.ppermute(observations[:, :HALO], "region", down)
-    own, w = own_gram(obs_count, obs_index, localization, observations)
-    return finish(obs_count, own, w, lower, upper, background, background_mean)
+    made = own_gram(*given)
+    after, *made = lax.optimization_barrier((observations, *made))
+    upper = lax.ppermute(after[:, :HALO], "region", down)
+    own, w = own_gram(*given, made)
+    own = upper_gram(own, w, upper)
+    return finish(obs_count, own, w, lower, background, background_mean)
 
 
 def solution(mesh):

time: 52.3 us -> 48.3 us (0.924)
  the two profiles are of different devices: /device:TPU:1 before, /device:TPU:128 now
where the time goes in v2:
time: 48.3 us; the launch traced here: 48 us
  starting transfers between devices  22.6 us (47%)
  Pallas kernels  20.6 us (43%)
  local copies, waits for them, and re-layouts  4.61 us (10%)
    ppermute x1, starting transfers between devices, on_device(): upper = lax.ppermute(after[:, :HALO], 'region', down)  17.4 us
    pallas_call x1, Pallas kernels, finish(): pl.pallas_call(finish_kernel, grid=(blocks // solve_batch,), out_shape=ja...  10.3 us
    pallas_call x2, Pallas kernels, own_gram(): pl.pallas_call(second_turn_kernel if made else first_turn_kernel, out_sha...  8.51 us
    ppermute x1, starting transfers between devices, on_device(): lower = lax.ppermute(observations[:, own_columns - HALO:], 'region', up)  5.19 us
    unnamed x12, local copies, waits for them, and re-layouts  3.58 us
    pallas_call x1, Pallas kernels, upper_gram(): pl.pallas_call(upper_gram_kernel, out_shape=jax.ShapeDtypeStruct(own.shap...  1.81 us
    slice x1, local copies, waits for them, and re-layouts, on_device(): lower = lax.ppermute(observations[:, own_columns - HALO:], 'region', up)  1.01 us
  transfers between devices with their start and end apart: 2, of which 0 were waited for; matrix products, arithmetic and copies ran while one was open for 0% of the time, Pallas kernels for 21%

profile of v2, /device:TPU:128, one launch (start us, length us, event | category | flops | bytes accessed | tf_op | source)
XLA Modules:
  0.0 48.0 jit_solution(9203462711703698398)
XLA Ops:
  0.0 1.0 %slice.7 = bf16[81,2048]{1,0:T(8,128)(2,1)S(1)} slice(bf16[81,4096]{1,0:T(8,128)(2,1)} %record.1), slice={[0:81], [2048:4096]} | slice | bytes 663552 | tf_op jit(solution)/shard_map/slice | solution.py:269
  1.0 5.2 %collective-permute-start.1 = (bf16[81,2048]{1,0:T(8,128)(2,1)S(1)}, bf16[81,2048]{1,0:T(8,128)(2,1)S(1)}, u32[]{:S(2)}, u32[]{:S(2)}) collective-permute-start(bf16[81,2048]{1,0:T(8,128)(2,1)S(1)} %slice.7), channel_id=1, source_target_pairs={{0,8},{8,16},{16,24},{24,32},{32,40},{40,48},{48,56},{56,64},{64,7... | collective-permute-start | bytes 995336 | tf_op jit(solution)/shard_map/ppermute | solution.py:269
  6.2 0.0 copy-start.1
  6.2 1.1 %copy-done.1 = bf16[81,4096]{1,0:T(8,128)(2,1)S(1)} copy-done((bf16[81,4096]{1,0:T(8,128)(2,1)S(1)}, bf16[81,4096]{1,0:T(8,128)(2,1)}, u32[]{:S(2)}) %copy-start.1) | copy-done | bytes 663576
  7.3 0.0 copy-start.3
  7.3 0.7 %copy-done.3 = s32[16]{0:T(128)S(1)} copy-done((s32[16]{0:T(128)S(1)}, s32[16]{0:T(128)}, u32[]{:S(2)}) %copy-start.3) | copy-done | bytes 88
  8.0 0.0 copy-start.4
  8.0 0.9 %copy-done.4 = s32[16,2048]{1,0:T(8,128)S(1)} copy-done((s32[16,2048]{1,0:T(8,128)S(1)}, s32[16,2048]{1,0:T(8,128)}, u32[]{:S(2)}) %copy-start.4) | copy-done | bytes 131096
  8.9 0.0 copy-start.5
  8.9 0.9 %copy-done.5 = f32[16,2048]{1,0:T(8,128)S(1)} copy-done((f32[16,2048]{1,0:T(8,128)S(1)}, f32[16,2048]{1,0:T(8,128)}, u32[]{:S(2)}) %copy-start.5) | copy-done | bytes 131096
  9.8 0.5 %own_gram_first.1 = (f32[1296,80]{1,0:T(8,128)S(1)}, f32[1024,128]{1,0:T(8,128)S(1)}) custom-call(s32[1]{0:T(128)} %bitcast.turn_ref, s32[16]{0:T(128)S(1)} %copy-done.3, s32[16,2048]{1,0:T(8,128)S(1)} %copy-done.4, f32[16,2048]{1,0:T(8,128)S(1)} %copy-done.5, bf16[81,4096]{1,0:T(8,128)(2,1)S(1)} %copy-done.1), custom_call_target="tpu_custom_call" | custom-call | flops 8000000000 | bytes 8000000 | tf_op jit(solution)/shard_map/own_gram_first/pallas_call | solution.py:103
  10.4 17.4 %collective-permute-start = (bf16[81,2048]{1,0:T(8,128)(2,1)S(1)}, bf16[81,2048]{1,0:T(8,128)(2,1)S(1)}, u32[]{:S(2)}, u32[]{:S(2)}) collective-permute-start(bf16[81,2048]{1,0:T(8,128)(2,1)S(1)} %slice.6), channel_id=1, source_target_pairs={{8,0},{16,8},{24,16},{32,24},{40,32},{48,40},{56,48},{64,56},{72,6... | collective-permute-start | bytes 995336 | tf_op jit(solution)/shard_map/ppermute | solution.py:272
  27.8 8.0 %own_gram_second.1 = (f32[1296,80]{1,0:T(8,128)S(1)}, f32[1024,128]{1,0:T(8,128)S(1)}) custom-call(s32[1]{0:T(128)} %bitcast.turn_ref, s32[16]{0:T(128)S(1)} %copy-done.3, s32[16,2048]{1,0:T(8,128)S(1)} %copy-done.4, f32[16,2048]{1,0:T(8,128)S(1)} %copy-done.5, bf16[81,4096]{1,0:T(8,128)(2,1)S(1)} %copy-done.1, ...), custom_call_target="tpu_custom_call", output_to_operand_aliasing={{0}: (5, {}), {1}: (6, {})} | custom-call | flops 8000000000 | bytes 8000000 | tf_op jit(solution)/shard_map/own_gram_second/pallas_call | solution.py:103
  35.8 0.0 collective-permute-done.upper_ref
  35.8 0.0 copy-start
  35.8 0.0 copy-start.2
  35.9 1.8 %upper_gram.1.own_ref = f32[1296,80]{1,0:T(8,128)S(1)} custom-call(f32[1296,80]{1,0:T(8,128)S(1)} %get-tuple-element.16.gram_in, f32[1024,128]{1,0:T(8,128)S(1)} %get-tuple-element.17.w_ref, bf16[81,2048]{1,0:T(8,128)(2,1)S(1)} %collective-permute-done.upper_ref), custom_call_target="tpu_custom_call", output_to_operand_aliasing={{}: (0, {})} | custom-call | flops 2000000000 | bytes 2000000 | tf_op jit(solution)/shard_map/upper_gram/pallas_call | solution.py:129
  37.7 0.0 collective-permute-done.1.lower_ref
  37.7 0.0 copy-done
  37.7 0.0 copy-done.2
  37.7 10.3 %finish.1 = bf16[16,80,512]{2,1,0:T(8,128)(2,1)} custom-call(s32[16]{0:T(128)S(1)} %copy-done.3, f32[1296,80]{1,0:T(8,128)S(1)} %upper_gram.1.own_ref, f32[1024,128]{1,0:T(8,128)S(1)} %get-tuple-element.17.w_ref, bf16[81,2048]{1,0:T(8,128)(2,1)S(1)} %collective-permute-done.1.lower_ref, bf16[16,80,512]{2,1,0:T(8,128)(2,1)S(1)} %copy-done, ...), custom_call_target="tpu_custom_call" | custom-call | tf_op jit(solution)/shard_map/finish/pallas_call | solution.py:242
  (1 shorter events, 0.0 us)
Async XLA Ops:
  1.0 36.7 %collective-permute-start.1 = (bf16[81,2048]{1,0:T(8,128)(2,1)S(1)}, bf16[81,2048]{1,0:T(8,128)(2,1)S(1)}, u32[]{:S(2)}, u32[]{:S(2)}) collective-permute-start(bf16[81,2048]{1,0:T(8,128)(2,1)S(1)} %slice.7), channel_id=1, source_target_pairs={{0,8},{8,16},{16,24},{24,32},{32,40},{40,48},{48,56},{56,64},{64,7... | collective-permute-start | bytes 995336 | tf_op jit(solution)/shard_map/ppermute | solution.py:269
  6.2 1.1 %copy-start.1 = (bf16[81,4096]{1,0:T(8,128)(2,1)S(1)}, bf16[81,4096]{1,0:T(8,128)(2,1)}, u32[]{:S(2)}) copy-start(bf16[81,4096]{1,0:T(8,128)(2,1)} %record.1) | copy-start | bytes 1990660
  7.3 0.7 %copy-start.3 = (s32[16]{0:T(128)S(1)}, s32[16]{0:T(128)}, u32[]{:S(2)}) copy-start(s32[16]{0:T(128)} %count_ref.1) | copy-start | bytes 196
  8.0 0.9 %copy-start.4 = (s32[16,2048]{1,0:T(8,128)S(1)}, s32[16,2048]{1,0:T(8,128)}, u32[]{:S(2)}) copy-start(s32[16,2048]{1,0:T(8,128)} %index.1) | copy-start | bytes 393220
  8.9 0.9 %copy-start.5 = (f32[16,2048]{1,0:T(8,128)S(1)}, f32[16,2048]{1,0:T(8,128)}, u32[]{:S(2)}) copy-start(f32[16,2048]{1,0:T(8,128)} %factor.1) | copy-start | bytes 393220
  10.4 25.4 %collective-permute-start = (bf16[81,2048]{1,0:T(8,128)(2,1)S(1)}, bf16[81,2048]{1,0:T(8,128)(2,1)S(1)}, u32[]{:S(2)}, u32[]{:S(2)}) collective-permute-start(bf16[81,2048]{1,0:T(8,128)(2,1)S(1)} %slice.6), channel_id=1, source_target_pairs={{8,0},{16,8},{24,16},{32,24},{40,32},{48,40},{56,48},{64,56},{72,6... | collective-permute-start | bytes 995336 | tf_op jit(solution)/shard_map/ppermute | solution.py:272
  35.8 1.9 %copy-start = (bf16[16,80,512]{2,1,0:T(8,128)(2,1)S(1)}, bf16[16,80,512]{2,1,0:T(8,128)(2,1)}, u32[]{:S(2)}) copy-start(bf16[16,80,512]{2,1,0:T(8,128)(2,1)} %background_ref.1) | copy-start | bytes 3932164
  35.8 1.8 %copy-start.2 = (f32[16,512]{1,0:T(8,128)S(1)}, f32[16,512]{1,0:T(8,128)}, u32[]{:S(2)}) copy-start(f32[16,512]{1,0:T(8,128)} %mean_ref.1) | copy-start | bytes 98308

commit v3 on v2

--- a/solution.py
+++ b/solution.py
@@ -10,7 +10,6 @@
 
 HALO = 2048
 NS_ITERS = 6
-RUN = 8
 LANES = 128
 BF16 = jnp.bfloat16
 F32 = jnp.float32
@@ -67,7 +66,7 @@
     lax.fori_loop(0, record_ref.shape[1] // width, step, 0)
 
 
-def own_gram_body(count_ref, index_ref, factor_ref, record_ref, gram_ref, w_ref):
+def own_gram_kernel(count_ref, index_ref, factor_ref, record_ref, gram_ref, w_ref):
     blocks = index_ref.shape[0]
 
     def step(i, carry):
@@ -80,64 +79,26 @@
     add_gram(record_ref, w_ref, HALO // LANES, blocks, gram_ref)
 
 
-def first_turn_kernel(turn_ref, *refs):
-    @pl.when(turn_ref[0] == 0)
-    def _():
-        own_gram_body(*refs)
-
-
-def second_turn_kernel(turn_ref, count, index, factor, record, gram_in, w_in, gram_ref, w_ref):
-    del gram_in, w_in
-
-    @pl.when(turn_ref[0] != 0)
-    def _():
-        own_gram_body(count, index, factor, record, gram_ref, w_ref)
-
-
-def own_gram(turn, obs_count, obs_index, localization, record, made=()):
+def own_gram(obs_count, obs_index, localization, record):
     blocks, p_most = obs_index.shape
     rows, columns = record.shape
     groups = (columns + 2 * HALO) // LANES
     smem = pl.BlockSpec(memory_space=pltpu.SMEM)
     vmem = pl.BlockSpec(memory_space=pltpu.VMEM)
     return pl.pallas_call(
-        second_turn_kernel if made else first_turn_kernel,
+        own_gram_kernel,
         out_shape=(
             jax.ShapeDtypeStruct((blocks * rows, rows - 1), F32),
             jax.ShapeDtypeStruct((groups * blocks, LANES), F32),
         ),
-        in_specs=[smem, smem, vmem, vmem, vmem] + [vmem] * len(made),
+        in_specs=[smem, vmem, vmem, vmem],
         out_specs=(vmem, vmem),
-        input_output_aliases={5: 0, 6: 1} if made else {},
         compiler_params=pltpu.CompilerParams(vmem_limit_bytes=40 * 2**20),
         cost_estimate=pl.CostEstimate(
             flops=8_000_000_000, bytes_accessed=8_000_000, transcendentals=0
         ),
-        name="own_gram_second" if made else "own_gram_first",
-    )(turn, obs_count, obs_index, localization, record, *made)
-
-
-def upper_gram_kernel(gram_in, w_ref, upper_ref, gram_ref):
-    blocks = gram_in.shape[0] // upper_ref.shape[0]
-    groups = w_ref.shape[0] // blocks
-    gram_ref[...] = gram_in[...]
-    add_gram(upper_ref, w_ref, groups - HALO // LANES, blocks, gram_ref)
-
-
-def upper_gram(own, w, upper):
-    vmem = pl.BlockSpec(memory_space=pltpu.VMEM)
-    return pl.pallas_call(
-        upper_gram_kernel,
-        out_shape=jax.ShapeDtypeStruct(own.shape, F32),
-        in_specs=[vmem, vmem, vmem],
-        out_specs=vmem,
-        input_output_aliases={0: 0},
-        compiler_params=pltpu.CompilerParams(vmem_limit_bytes=40 * 2**20),
-        cost_estimate=pl.CostEstimate(
-            flops=2_000_000_000, bytes_accessed=2_000_000, transcendentals=0
-        ),
-        name="upper_gram",
-    )(own, w, upper)
+        name="own_gram",
+    )(obs_count, obs_index, localization, record)
 
 
 def padded(x):
@@ -208,7 +169,16 @@
 
 
 def finish_kernel(
-    count_ref, own_ref, w_ref, lower_ref, background_ref, mean_ref, out_ref, gram_ref
+    count_ref,
+    odd_ref,
+    own_ref,
+    w_ref,
+    far_ref,
+    near_ref,
+    background_ref,
+    mean_ref,
+    out_ref,
+    gram_ref,
 ):
     step = pl.program_id(0)
     blocks = count_ref.shape[0]
@@ -217,7 +187,10 @@
     @pl.when(step == 0)
     def _():
         gram_ref[...] = own_ref[...]
-        add_gram(lower_ref, w_ref, 0, blocks, gram_ref)
+        upper = w_ref.shape[0] // blocks - HALO // LANES
+        odd = odd_ref[0]
+        add_gram(near_ref, w_ref, odd * upper, blocks, gram_ref)
+        add_gram(far_ref, w_ref, (1 - odd) * upper, blocks, gram_ref)
 
     informations, innovations = [], []
     for i in range(solve_batch):
@@ -232,7 +205,7 @@
         out_ref[i] = (mean_ref[pl.ds(b, 1), :] + mixed).astype(BF16)
 
 
-def finish(obs_count, own, w, lower, background, background_mean):
+def finish(obs_count, odd, own, w, far, near, background, background_mean):
     blocks, members, cells = background.shape
 
     def whole(x):
@@ -245,9 +218,11 @@
         out_shape=jax.ShapeDtypeStruct(background.shape, BF16),
         in_specs=[
             pl.BlockSpec(memory_space=pltpu.SMEM),
+            pl.BlockSpec(memory_space=pltpu.SMEM),
             whole(own),
             whole(w),
-            whole(lower),
+            whole(far),
+            whole(near),
             states,
             whole(background_mean),
         ],
@@ -255,24 +230,28 @@
         scratch_shapes=[pltpu.VMEM(own.shape, F32)],
         compiler_params=pltpu.CompilerParams(vmem_limit_bytes=40 * 2**20),
         name="finish",
-    )(obs_count, own, w, lower, background, background_mean)
+    )(obs_count, odd, own, w, far, near, background, background_mean)
 
 
 def on_device(observations, obs_index, obs_count, localization, background, background_mean):
     count = lax.axis_size("region")
-    up = [(i, (i + 1) % count) for i in range(count)]
-    down = [(j, i) for i, j in up]
-    own_columns = observations.shape[1]
-    place = lax.axis_index("region")
-    turn = jnp.minimum(place % RUN, 1).astype(jnp.int32)[None]
-    given = (turn, obs_count, obs_index, localization, observations)
-    lower = lax.ppermute(observations[:, own_columns - HALO :], "region", up)
-    made = own_gram(*given)
-    after, *made = lax.optimization_barrier((observations, *made))
-    upper = lax.ppermute(after[:, :HALO], "region", down)
-    own, w = own_gram(*given, made)
-    own = upper_gram(own, w, upper)
-    return finish(obs_count, own, w, lower, background, background_mean)
+    odd = lax.axis_index("region") % 2
+
+    def swap(record, parity):
+        below = record[:, :HALO]
+        above = record[:, record.shape[1] - HALO :]
+        sent = jnp.where(odd == parity, above, below)
+        pairs = [((2 * i + parity) % count, (2 * i + 1 + parity) % count) for i in range(count // 2)]
+        pairs += [(j, i) for i, j in pairs]
+        return sent, pairs
+
+    sent_1, pairs_1 = swap(observations, 1)
+    sent_2, pairs_2 = swap(observations, 0)
+    far = lax.ppermute(sent_2, "region", pairs_2)
+    near = lax.ppermute(sent_1, "region", pairs_1)
+    own, w = own_gram(obs_count, obs_index, localization, observations)
+    odd = odd.astype(jnp.int32)[None]
+    return finish(obs_count, odd, own, w, far, near, background, background_mean)
 
 
 def solution(mesh):

time: 48.3 us -> 46.1 us (0.954)
  the two profiles are of different devices: /device:TPU:128 before, /device:TPU:1 now
where the time goes in v3:
time: 46.1 us; the launch traced here: 45.6 us
  starting transfers between devices  23.4 us (51%)
  Pallas kernels  20 us (43%)
  other arithmetic  1.22 us (3%)
  waiting for transfers between devices  0.91 us (2%)
    ppermute x1, starting transfers between devices, on_device(): near = lax.ppermute(sent_1, 'region', pairs_1)  21.3 us
    pallas_call x1, Pallas kernels, finish(): pl.pallas_call(finish_kernel, grid=(blocks // solve_batch,), out_shape=ja...  12 us
    pallas_call x1, Pallas kernels, own_gram(): pl.pallas_call(own_gram_kernel, out_shape=(jax.ShapeDtypeStruct((blocks *...  7.96 us
    ppermute x1, starting transfers between devices, on_device(): far = lax.ppermute(sent_2, 'region', pairs_2)  2.05 us
    select_n x1, other arithmetic, swap(): sent = jnp.where(odd == parity, above, below)  1.22 us
  transfers between devices with their start and end apart: 2, of which 1 were waited for; matrix products, arithmetic and copies ran while one was open for 0% of the time, Pallas kernels for 17%

profile of v3, /device:TPU:1, one launch (start us, length us, event | category | flops | bytes accessed | tf_op | source)
XLA Modules:
  0.0 45.6 jit_solution(11409995457395885949)
XLA Ops:
  0.0 0.0 copy-start.1
  0.0 0.0 copy-start.3
  0.0 0.0 copy-start.5
  0.0 0.0 copy-start.4
  0.0 1.2 %broadcast_select_fusion = (bf16[81,2048]{1,0:T(8,128)(2,1)S(1)}, bf16[81,2048]{1,0:T(8,128)(2,1)S(1)}) fusion(pred[]{:T(512)S(6)} %eq.9, bf16[81,4096]{1,0:T(8,128)(2,1)} %record_ref.1, pred[]{:T(512)S(6)} %eq.8), kind=kLoop, calls=%fused_computation | loop fusion | flops 331776 | bytes 1327106 | tf_op jit(solution)/shard_map/jit(_where)/select_n | solution.py:243
  1.3 21.3 %collective-permute-start.1 = (bf16[81,2048]{1,0:T(8,128)(2,1)S(1)}, bf16[81,2048]{1,0:T(8,128)(2,1)S(1)}, u32[]{:S(2)}, u32[]{:S(2)}) collective-permute-start(bf16[81,2048]{1,0:T(8,128)(2,1)S(1)} %get-tuple-element.9), channel_id=1, source_target_pairs={{8,16},{24,32},{40,48},{56,64},{72,80},{88,96},{104,112},{120,128}... | collective-permute-start | bytes 995336 | tf_op jit(solution)/shard_map/ppermute | solution.py:251
  22.6 0.0 copy-start
  22.6 0.0 copy-start.2
  22.6 2.1 %collective-permute-start = (bf16[81,2048]{1,0:T(8,128)(2,1)S(1)}, bf16[81,2048]{1,0:T(8,128)(2,1)S(1)}, u32[]{:S(2)}, u32[]{:S(2)}) collective-permute-start(bf16[81,2048]{1,0:T(8,128)(2,1)S(1)} %get-tuple-element.10), channel_id=1, source_target_pairs={{0,8},{16,24},{32,40},{48,56},{64,72},{80,88},{96,104},{112,120},{... | collective-permute-start | bytes 995336 | tf_op jit(solution)/shard_map/ppermute | solution.py:250
  24.7 0.0 copy-done.1
  24.7 0.0 copy-done.3
  24.7 0.0 copy-done.5
  24.7 0.0 copy-done.4
  24.7 8.0 %own_gram.1 = (f32[1296,80]{1,0:T(8,128)S(1)}, f32[1024,128]{1,0:T(8,128)S(1)}) custom-call(s32[16]{0:T(128)S(1)} %copy-done.3, s32[16,2048]{1,0:T(8,128)S(1)} %copy-done.4, f32[16,2048]{1,0:T(8,128)S(1)} %copy-done.5, bf16[81,4096]{1,0:T(8,128)(2,1)S(1)} %copy-done.1), custom_call_target="tpu_custom_call" | custom-call | flops 8000000000 | bytes 8000000 | tf_op jit(solution)/shard_map/own_gram/pallas_call | solution.py:88
  32.7 0.0 collective-permute-done.1.near_ref
  32.7 0.9 %collective-permute-done.far_ref = bf16[81,2048]{1,0:T(8,128)(2,1)S(1)} collective-permute-done((bf16[81,2048]{1,0:T(8,128)(2,1)S(1)}, bf16[81,2048]{1,0:T(8,128)(2,1)S(1)}, u32[]{:S(2)}, u32[]{:S(2)}) %collective-permute-start) | collective-permute-done | bytes 331808 | tf_op jit(solution)/shard_map/ppermute | solution.py:250
  33.6 0.0 copy-done
  33.6 0.0 copy-done.2
  33.6 12.0 %finish.1 = bf16[16,80,512]{2,1,0:T(8,128)(2,1)} custom-call(s32[16]{0:T(128)S(1)} %copy-done.3, s32[1]{0:T(128)} %bitcast.odd_ref, f32[1296,80]{1,0:T(8,128)S(1)} %get-tuple-element.7.own_ref, f32[1024,128]{1,0:T(8,128)S(1)} %get-tuple-element.8.w_ref, bf16[81,2048]{1,0:T(8,128)(2,1)S(1)} %collective-permute-done.far_ref, ...), custom_call_target="tpu_custom_call" | custom-call | tf_op jit(solution)/shard_map/finish/pallas_call | solution.py:215
Async XLA Ops:
  0.0 24.7 %copy-start.1 = (bf16[81,4096]{1,0:T(8,128)(2,1)S(1)}, bf16[81,4096]{1,0:T(8,128)(2,1)}, u32[]{:S(2)}) copy-start(bf16[81,4096]{1,0:T(8,128)(2,1)} %record_ref.1) | copy-start | bytes 1990660
  0.0 24.7 %copy-start.3 = (s32[16]{0:T(128)S(1)}, s32[16]{0:T(128)}, u32[]{:S(2)}) copy-start(s32[16]{0:T(128)} %count_ref.3) | copy-start | bytes 196
  0.0 24.7 %copy-start.5 = (f32[16,2048]{1,0:T(8,128)S(1)}, f32[16,2048]{1,0:T(8,128)}, u32[]{:S(2)}) copy-start(f32[16,2048]{1,0:T(8,128)} %factor_ref.1) | copy-start | bytes 393220
  0.0 24.7 %copy-start.4 = (s32[16,2048]{1,0:T(8,128)S(1)}, s32[16,2048]{1,0:T(8,128)}, u32[]{:S(2)}) copy-start(s32[16,2048]{1,0:T(8,128)} %index_ref.1) | copy-start | bytes 393220
  1.3 31.4 %collective-permute-start.1 = (bf16[81,2048]{1,0:T(8,128)(2,1)S(1)}, bf16[81,2048]{1,0:T(8,128)(2,1)S(1)}, u32[]{:S(2)}, u32[]{:S(2)}) collective-permute-start(bf16[81,2048]{1,0:T(8,128)(2,1)S(1)} %get-tuple-element.9), channel_id=1, source_target_pairs={{8,16},{24,32},{40,48},{56,64},{72,80},{88,96},{104,112},{120,128}... | collective-permute-start | bytes 995336 | tf_op jit(solution)/shard_map/ppermute | solution.py:251
  22.6 11.0 %copy-start = (bf16[16,80,512]{2,1,0:T(8,128)(2,1)S(1)}, bf16[16,80,512]{2,1,0:T(8,128)(2,1)}, u32[]{:S(2)}) copy-start(bf16[16,80,512]{2,1,0:T(8,128)(2,1)} %background_ref.1) | copy-start | bytes 3932164
  22.6 11.0 %copy-start.2 = (f32[16,512]{1,0:T(8,128)S(1)}, f32[16,512]{1,0:T(8,128)}, u32[]{:S(2)}) copy-start(f32[16,512]{1,0:T(8,128)} %mean_ref.1) | copy-start | bytes 98308
  22.6 11.0 %collective-permute-start = (bf16[81,2048]{1,0:T(8,128)(2,1)S(1)}, bf16[81,2048]{1,0:T(8,128)(2,1)S(1)}, u32[]{:S(2)}, u32[]{:S(2)}) collective-permute-start(bf16[81,2048]{1,0:T(8,128)(2,1)S(1)} %get-tuple-element.10), channel_id=1, source_target_pairs={{0,8},{16,24},{32,40},{48,56},{64,72},{80,88},{96,104},{112,120},{... | collective-permute-start | bytes 995336 | tf_op jit(solution)/shard_map/ppermute | solution.py:250

commit v4 on v2

--- a/solution.py
+++ b/solution.py
@@ -117,17 +117,15 @@
     )(turn, obs_count, obs_index, localization, record, *made)
 
 
-def upper_gram_kernel(gram_in, w_ref, upper_ref, gram_ref):
-    blocks = gram_in.shape[0] // upper_ref.shape[0]
-    groups = w_ref.shape[0] // blocks
+def lower_gram_kernel(gram_in, w_ref, lower_ref, gram_ref):
     gram_ref[...] = gram_in[...]
-    add_gram(upper_ref, w_ref, groups - HALO // LANES, blocks, gram_ref)
-
-
-def upper_gram(own, w, upper):
+    add_gram(lower_ref, w_ref, 0, gram_in.shape[0] // lower_ref.shape[0], gram_ref)
+
+
+def lower_gram(own, w, lower):
     vmem = pl.BlockSpec(memory_space=pltpu.VMEM)
     return pl.pallas_call(
-        upper_gram_kernel,
+        lower_gram_kernel,
         out_shape=jax.ShapeDtypeStruct(own.shape, F32),
         in_specs=[vmem, vmem, vmem],
         out_specs=vmem,
@@ -136,8 +134,8 @@
         cost_estimate=pl.CostEstimate(
             flops=2_000_000_000, bytes_accessed=2_000_000, transcendentals=0
         ),
-        name="upper_gram",
-    )(own, w, upper)
+        name="lower_gram",
+    )(own, w, lower)
 
 
 def padded(x):
@@ -208,7 +206,7 @@
 
 
 def finish_kernel(
-    count_ref, own_ref, w_ref, lower_ref, background_ref, mean_ref, out_ref, gram_ref
+    count_ref, own_ref, w_ref, upper_ref, background_ref, mean_ref, out_ref, gram_ref
 ):
     step = pl.program_id(0)
     blocks = count_ref.shape[0]
@@ -217,7 +215,8 @@
     @pl.when(step == 0)
     def _():
         gram_ref[...] = own_ref[...]
-        add_gram(lower_ref, w_ref, 0, blocks, gram_ref)
+        groups = w_ref.shape[0] // blocks
+        add_gram(upper_ref, w_ref, groups - HALO // LANES, blocks, gram_ref)
 
     informations, innovations = [], []
     for i in range(solve_batch):
@@ -232,7 +231,7 @@
         out_ref[i] = (mean_ref[pl.ds(b, 1), :] + mixed).astype(BF16)
 
 
-def finish(obs_count, own, w, lower, background, background_mean):
+def finish(obs_count, own, w, upper, background, background_mean):
     blocks, members, cells = background.shape
 
     def whole(x):
@@ -247,7 +246,7 @@
             pl.BlockSpec(memory_space=pltpu.SMEM),
             whole(own),
             whole(w),
-            whole(lower),
+            whole(upper),
             states,
             whole(background_mean),
         ],
@@ -255,7 +254,7 @@
         scratch_shapes=[pltpu.VMEM(own.shape, F32)],
         compiler_params=pltpu.CompilerParams(vmem_limit_bytes=40 * 2**20),
         name="finish",
-    )(obs_count, own, w, lower, background, background_mean)
+    )(obs_count, own, w, upper, background, background_mean)
 
 
 def on_device(observations, obs_index, obs_count, localization, background, background_mean):
@@ -268,11 +267,11 @@
     given = (turn, obs_count, obs_index, localization, observations)
     lower = lax.ppermute(observations[:, own_columns - HALO :], "region", up)
     made = own_gram(*given)
-    after, *made = lax.optimization_barrier((observations, *made))
-    upper = lax.ppermute(after[:, :HALO], "region", down)
+    first, *made = lax.optimization_barrier((observations[:, :HALO], *made))
+    upper = lax.ppermute(first, "region", down)
     own, w = own_gram(*given, made)
-    own = upper_gram(own, w, upper)
-    return finish(obs_count, own, w, lower, background, background_mean)
+    own = lower_gram(own, w, lower)
+    return finish(obs_count, own, w, upper, background, background_mean)
 
 
 def solution(mesh):

time: 48.3 us -> 44.9 us (0.930)
  local copies, waits for them, and re-layouts: 4.61 us -> 1.25 us
    unnamed x12, local copies, waits for them, and re-layouts: 3.58 us -> 0.03 us
  transfers between devices with their start and end apart: 2 -> 2, of which waited for: 0 -> 0; matrix products, arithmetic and copies ran while one was open for 0% -> 0% of each run, Pallas kernels for 21% -> 23%
where the time goes in v4:
time: 44.9 us; the launch traced here: 44.7 us
  starting transfers between devices  22.6 us (50%)
  Pallas kernels  20.7 us (46%)
  local copies, waits for them, and re-layouts  1.25 us (3%)
    ppermute x1, starting transfers between devices, on_device(): upper = lax.ppermute(first, 'region', down)  17.4 us
    pallas_call x1, Pallas kernels, finish(): pl.pallas_call(finish_kernel, grid=(blocks // solve_batch,), out_shape=ja...  10.3 us
    pallas_call x2, Pallas kernels, own_gram(): pl.pallas_call(second_turn_kernel if made else first_turn_kernel, out_sha...  8.52 us
    ppermute x1, starting transfers between devices, on_device(): lower = lax.ppermute(observations[:, own_columns - HALO:], 'region', up)  5.19 us
    pallas_call x1, Pallas kernels, lower_gram(): pl.pallas_call(lower_gram_kernel, out_shape=jax.ShapeDtypeStruct(own.shap...  1.81 us
    slice x1, local copies, waits for them, and re-layouts, on_device(): lower = lax.ppermute(observations[:, own_columns - HALO:], 'region', up)  1.22 us
  transfers between devices with their start and end apart: 2, of which 0 were waited for; matrix products, arithmetic and copies ran while one was open for 0% of the time, Pallas kernels for 23%

profile of v4, /device:TPU:128, one launch (start us, length us, event | category | flops | bytes accessed | tf_op | source)
XLA Modules:
  0.0 44.7 jit_solution(2500234506853721230)
XLA Ops:
  0.0 0.0 copy-start.1
  0.0 0.0 copy-start.3
  0.0 0.0 copy-start.5
  0.0 0.0 copy-start.4
  0.0 1.2 %fusion = (bf16[81,2048]{1,0:T(8,128)(2,1)S(1)}, bf16[81,2048]{1,0:T(8,128)(2,1)S(1)}) fusion(bf16[81,4096]{1,0:T(8,128)(2,1)} %record.1), kind=kLoop, calls=%fused_computation | loop fusion | bytes 1327104 | tf_op jit(solution)/shard_map/slice | solution.py:268
  1.2 5.2 %collective-permute-start = (bf16[81,2048]{1,0:T(8,128)(2,1)S(1)}, bf16[81,2048]{1,0:T(8,128)(2,1)S(1)}, u32[]{:S(2)}, u32[]{:S(2)}) collective-permute-start(bf16[81,2048]{1,0:T(8,128)(2,1)S(1)} %get-tuple-element.19), channel_id=1, source_target_pairs={{0,8},{8,16},{16,24},{24,32},{32,40},{40,48},{48,56},{56,64},{64,7... | collective-permute-start | bytes 995336 | tf_op jit(solution)/shard_map/ppermute | solution.py:268
  6.5 0.0 copy-done.1
  6.5 0.0 copy-done.3
  6.5 0.0 copy-done.5
  6.5 0.0 copy-done.4
  6.5 0.5 %own_gram_first.1 = (f32[1296,80]{1,0:T(8,128)S(1)}, f32[1024,128]{1,0:T(8,128)S(1)}) custom-call(s32[1]{0:T(128)} %bitcast.turn_ref, s32[16]{0:T(128)S(1)} %copy-done.3, s32[16,2048]{1,0:T(8,128)S(1)} %copy-done.4, f32[16,2048]{1,0:T(8,128)S(1)} %copy-done.5, bf16[81,4096]{1,0:T(8,128)(2,1)S(1)} %copy-done.1), custom_call_target="tpu_custom_call" | custom-call | flops 8000000000 | bytes 8000000 | tf_op jit(solution)/shard_map/own_gram_first/pallas_call | solution.py:103
  7.1 17.4 %collective-permute-start.1 = (bf16[81,2048]{1,0:T(8,128)(2,1)S(1)}, bf16[81,2048]{1,0:T(8,128)(2,1)S(1)}, u32[]{:S(2)}, u32[]{:S(2)}) collective-permute-start(bf16[81,2048]{1,0:T(8,128)(2,1)S(1)} %get-tuple-element.18), channel_id=1, source_target_pairs={{8,0},{16,8},{24,16},{32,24},{40,32},{48,40},{56,48},{64,56},{72,6... | collective-permute-start | bytes 995336 | tf_op jit(solution)/shard_map/ppermute | solution.py:271
  24.5 8.0 %own_gram_second.1 = (f32[1296,80]{1,0:T(8,128)S(1)}, f32[1024,128]{1,0:T(8,128)S(1)}) custom-call(s32[1]{0:T(128)} %bitcast.turn_ref, s32[16]{0:T(128)S(1)} %copy-done.3, s32[16,2048]{1,0:T(8,128)S(1)} %copy-done.4, f32[16,2048]{1,0:T(8,128)S(1)} %copy-done.5, bf16[81,4096]{1,0:T(8,128)(2,1)S(1)} %copy-done.1, ...), custom_call_target="tpu_custom_call", output_to_operand_aliasing={{0}: (5, {}), {1}: (6, {})} | custom-call | flops 8000000000 | bytes 8000000 | tf_op jit(solution)/shard_map/own_gram_second/pallas_call | solution.py:103
  32.5 0.0 collective-permute-done.lower_ref
  32.5 0.0 copy-start
  32.5 0.0 copy-start.2
  32.5 1.8 %lower_gram.1.own_ref = f32[1296,80]{1,0:T(8,128)S(1)} custom-call(f32[1296,80]{1,0:T(8,128)S(1)} %get-tuple-element.16.gram_in, f32[1024,128]{1,0:T(8,128)S(1)} %get-tuple-element.17.w_ref, bf16[81,2048]{1,0:T(8,128)(2,1)S(1)} %collective-permute-done.lower_ref), custom_call_target="tpu_custom_call", output_to_operand_aliasing={{}: (0, {})} | custom-call | flops 2000000000 | bytes 2000000 | tf_op jit(solution)/shard_map/lower_gram/pallas_call | solution.py:127
  34.3 0.0 collective-permute-done.1.upper_ref
  34.3 0.0 copy-done
  34.4 0.0 copy-done.2
  34.4 10.3 %finish.1 = bf16[16,80,512]{2,1,0:T(8,128)(2,1)} custom-call(s32[16]{0:T(128)S(1)} %copy-done.3, f32[1296,80]{1,0:T(8,128)S(1)} %lower_gram.1.own_ref, f32[1024,128]{1,0:T(8,128)S(1)} %get-tuple-element.17.w_ref, bf16[81,2048]{1,0:T(8,128)(2,1)S(1)} %collective-permute-done.1.upper_ref, bf16[16,80,512]{2,1,0:T(8,128)(2,1)S(1)} %copy-done, ...), custom_call_target="tpu_custom_call" | custom-call | tf_op jit(solution)/shard_map/finish/pallas_call | solution.py:241
Async XLA Ops:
  0.0 6.5 %copy-start.1 = (bf16[81,4096]{1,0:T(8,128)(2,1)S(1)}, bf16[81,4096]{1,0:T(8,128)(2,1)}, u32[]{:S(2)}) copy-start(bf16[81,4096]{1,0:T(8,128)(2,1)} %record.1) | copy-start | bytes 1990660
  0.0 6.5 %copy-start.3 = (s32[16]{0:T(128)S(1)}, s32[16]{0:T(128)}, u32[]{:S(2)}) copy-start(s32[16]{0:T(128)} %count_ref.1) | copy-start | bytes 196
  0.0 6.5 %copy-start.5 = (f32[16,2048]{1,0:T(8,128)S(1)}, f32[16,2048]{1,0:T(8,128)}, u32[]{:S(2)}) copy-start(f32[16,2048]{1,0:T(8,128)} %factor.1) | copy-start | bytes 393220
  0.0 6.5 %copy-start.4 = (s32[16,2048]{1,0:T(8,128)S(1)}, s32[16,2048]{1,0:T(8,128)}, u32[]{:S(2)}) copy-start(s32[16,2048]{1,0:T(8,128)} %index.1) | copy-start | bytes 393220
  1.2 31.2 %collective-permute-start = (bf16[81,2048]{1,0:T(8,128)(2,1)S(1)}, bf16[81,2048]{1,0:T(8,128)(2,1)S(1)}, u32[]{:S(2)}, u32[]{:S(2)}) collective-permute-start(bf16[81,2048]{1,0:T(8,128)(2,1)S(1)} %get-tuple-element.19), channel_id=1, source_target_pairs={{0,8},{8,16},{16,24},{24,32},{32,40},{40,48},{48,56},{56,64},{64,7... | collective-permute-start | bytes 995336 | tf_op jit(solution)/shard_map/ppermute | solution.py:268
  7.1 27.3 %collective-permute-start.1 = (bf16[81,2048]{1,0:T(8,128)(2,1)S(1)}, bf16[81,2048]{1,0:T(8,128)(2,1)S(1)}, u32[]{:S(2)}, u32[]{:S(2)}) collective-permute-start(bf16[81,2048]{1,0:T(8,128)(2,1)S(1)} %get-tuple-element.18), channel_id=1, source_target_pairs={{8,0},{16,8},{24,16},{32,24},{40,32},{48,40},{56,48},{64,56},{72,6... | collective-permute-start | bytes 995336 | tf_op jit(solution)/shard_map/ppermute | solution.py:271
  32.5 1.9 %copy-start = (bf16[16,80,512]{2,1,0:T(8,128)(2,1)S(1)}, bf16[16,80,512]{2,1,0:T(8,128)(2,1)}, u32[]{:S(2)}) copy-start(bf16[16,80,512]{2,1,0:T(8,128)(2,1)} %background_ref.1) | copy-start | bytes 3932164
  32.5 1.8 %copy-start.2 = (f32[16,512]{1,0:T(8,128)S(1)}, f32[16,512]{1,0:T(8,128)}, u32[]{:S(2)}) copy-start(f32[16,512]{1,0:T(8,128)} %mean_ref.1) | copy-start | bytes 98308

commit v5 on v4

--- a/solution.py
+++ b/solution.py
@@ -18,7 +18,6 @@
 
 hist_unroll = 2
 gram_chunk = 8
-solve_batch = 8
 
 
 def histogram(block, count_ref, index_ref, factor_ref, w_ref):
@@ -148,19 +147,14 @@
 
 
 def right_terms(x):
-    upper, lower = terms(x)
-    rest = jnp.zeros((LANES - x.shape[0], LANES), BF16)
-    return (
-        jnp.concatenate([upper, rest, upper, rest], axis=0),
-        jnp.concatenate([lower, rest], axis=0),
-    )
+    both = jnp.concatenate(terms(x), axis=1)
+    half = jnp.concatenate([both, jnp.zeros((LANES - x.shape[0], 2 * LANES), BF16)], axis=0)
+    return jnp.concatenate([half, half], axis=0)
 
 
 def multiply(x, right):
-    upper, lower = terms(x)
-    return jnp.dot(
-        jnp.concatenate([upper, lower], axis=1), right[0], preferred_element_type=F32
-    ) + jnp.dot(upper, right[1], preferred_element_type=F32)
+    product = jnp.dot(jnp.concatenate(terms(x), axis=1), right, preferred_element_type=F32)
+    return product[:, :LANES] + product[:, LANES:]
 
 
 def solve_blocks(informations, innovations):
@@ -206,52 +200,49 @@
 
 
 def finish_kernel(
-    count_ref, own_ref, w_ref, upper_ref, background_ref, mean_ref, out_ref, gram_ref
+    count_ref,
+    own_ref,
+    w_ref,
+    upper_ref,
+    background_ref,
+    mean_ref,
+    out_ref,
+    gram_ref,
+    made_ref,
+    sems,
 ):
-    step = pl.program_id(0)
-    blocks = count_ref.shape[0]
-    members = background_ref.shape[1]
-
-    @pl.when(step == 0)
-    def _():
-        gram_ref[...] = own_ref[...]
-        groups = w_ref.shape[0] // blocks
-        add_gram(upper_ref, w_ref, groups - HALO // LANES, blocks, gram_ref)
-
-    informations, innovations = [], []
-    for i in range(solve_batch):
-        b = step * solve_batch + i
-        informations.append(gram_ref[pl.ds(pl.multiple_of(b * members, members), members), :])
-        innovations.append(gram_ref[pl.ds(blocks * members + b, 1), :])
+    blocks, members, _ = background_ref.shape
+    groups = w_ref.shape[0] // blocks
+    gram_ref[...] = own_ref[...]
+    add_gram(upper_ref, w_ref, groups - HALO // LANES, blocks, gram_ref)
+    informations = [gram_ref[b * members : (b + 1) * members, :] for b in range(blocks)]
+    at = blocks * members
+    innovations = [gram_ref[at + b : at + b + 1, :] for b in range(blocks)]
     solved, eye = solve_blocks(informations, innovations)
-    for i in range(solve_batch):
-        b = step * solve_batch + i
-        weights = jnp.where(count_ref[b] > 0, solved[i], eye).astype(BF16)
-        mixed = jnp.dot(weights, background_ref[i], preferred_element_type=F32)
-        out_ref[i] = (mean_ref[pl.ds(b, 1), :] + mixed).astype(BF16)
+    copies = []
+    for b in range(blocks):
+        weights = jnp.where(count_ref[b] > 0, solved[b], eye).astype(BF16)
+        mixed = jnp.dot(weights, background_ref[b], preferred_element_type=F32)
+        made_ref[b] = (mean_ref[b : b + 1, :] + mixed).astype(BF16)
+        copies.append(pltpu.make_async_copy(made_ref.at[b], out_ref.at[b], sems.at[b]))
+        copies[b].start()
+    for copy in copies:
+        copy.wait()
 
 
 def finish(obs_count, own, w, upper, background, background_mean):
-    blocks, members, cells = background.shape
-
-    def whole(x):
-        return pl.BlockSpec(x.shape, lambda i: (0,) * x.ndim)
-
-    states = pl.BlockSpec((solve_batch, members, cells), lambda i: (i, 0, 0))
+    blocks = background.shape[0]
+    vmem = pl.BlockSpec(memory_space=pltpu.VMEM)
     return pl.pallas_call(
         finish_kernel,
-        grid=(blocks // solve_batch,),
         out_shape=jax.ShapeDtypeStruct(background.shape, BF16),
-        in_specs=[
-            pl.BlockSpec(memory_space=pltpu.SMEM),
-            whole(own),
-            whole(w),
-            whole(upper),
-            states,
-            whole(background_mean),
+        in_specs=[pl.BlockSpec(memory_space=pltpu.SMEM)] + [vmem] * 5,
+        out_specs=pl.BlockSpec(memory_space=pl.ANY),
+        scratch_shapes=[
+            pltpu.VMEM(own.shape, F32),
+            pltpu.VMEM(background.shape, BF16),
+            pltpu.SemaphoreType.DMA((blocks,)),
         ],
-        out_specs=states,
-        scratch_shapes=[pltpu.VMEM(own.shape, F32)],
         compiler_params=pltpu.CompilerParams(vmem_limit_bytes=40 * 2**20),
         name="finish",
     )(obs_count, own, w, upper, background, background_mean)
@@ -263,7 +254,7 @@
     down = [(j, i) for i, j in up]
     own_columns = observations.shape[1]
     place = lax.axis_index("region")
-    turn = jnp.minimum(place % RUN, 1).astype(jnp.int32)[None]
+    turn = jnp.minimum(place % RUN // 2, 1).astype(jnp.int32)[None]
     given = (turn, obs_count, obs_index, localization, observations)
     lower = lax.ppermute(observations[:, own_columns - HALO :], "region", up)
     made = own_gram(*given)

time: 44.9 us -> 39.8 us (0.89)
  the two profiles are of different devices: /device:TPU:128 before, /device:TPU:1 now
where the time goes in v5:
time: 39.8 us; the launch traced here: 39.7 us
  Pallas kernels  17.5 us (44%)
  starting transfers between devices  15.8 us (40%)
  waiting for transfers between devices  4.97 us (12%)
  local copies, waits for them, and re-layouts  1.25 us (3%)
    ppermute x1, starting transfers between devices, on_device(): upper = lax.ppermute(first, 'region', down)  10.1 us
    pallas_call x2, Pallas kernels, own_gram(): pl.pallas_call(second_turn_kernel if made else first_turn_kernel, out_sha...  8.52 us
    pallas_call x1, Pallas kernels, finish(): pl.pallas_call(finish_kernel, out_shape=jax.ShapeDtypeStruct(background.s...  7.18 us
    ppermute x1, starting transfers between devices, on_device(): lower = lax.ppermute(observations[:, own_columns - HALO:], 'region', up)  5.74 us
    ppermute x1, waiting for transfers between devices, on_device(): lower = lax.ppermute(observations[:, own_columns - HALO:], 'region', up)  4.97 us
    pallas_call x1, Pallas kernels, lower_gram(): pl.pallas_call(lower_gram_kernel, out_shape=jax.ShapeDtypeStruct(own.shap...  1.81 us
    slice x1, local copies, waits for them, and re-layouts, on_device(): lower = lax.ppermute(observations[:, own_columns - HALO:], 'region', up)  1.22 us
  transfers between devices with their start and end apart: 2, of which 1 were waited for; matrix products, arithmetic and copies ran while one was open for 0% of the time, Pallas kernels for 26%

profile of v5, /device:TPU:1, one launch (start us, length us, event | category | flops | bytes accessed | tf_op | source)
XLA Modules:
  0.0 39.7 jit_solution(16870525445126872612)
XLA Ops:
  0.0 0.0 copy-start.1
  0.0 0.0 copy-start.3
  0.0 0.0 copy-start.5
  0.0 0.0 copy-start.4
  0.0 1.2 %fusion = (bf16[81,2048]{1,0:T(8,128)(2,1)S(1)}, bf16[81,2048]{1,0:T(8,128)(2,1)S(1)}) fusion(bf16[81,4096]{1,0:T(8,128)(2,1)} %record.1), kind=kLoop, calls=%fused_computation | loop fusion | bytes 1327104 | tf_op jit(solution)/shard_map/slice | solution.py:259
  1.2 5.7 %collective-permute-start = (bf16[81,2048]{1,0:T(8,128)(2,1)S(1)}, bf16[81,2048]{1,0:T(8,128)(2,1)S(1)}, u32[]{:S(2)}, u32[]{:S(2)}) collective-permute-start(bf16[81,2048]{1,0:T(8,128)(2,1)S(1)} %get-tuple-element.19), channel_id=1, source_target_pairs={{0,8},{8,16},{16,24},{24,32},{32,40},{40,48},{48,56},{56,64},{64,7... | collective-permute-start | bytes 995336 | tf_op jit(solution)/shard_map/ppermute | solution.py:259
  7.0 0.0 copy-done.1
  7.0 0.0 copy-done.3
  7.0 0.0 copy-done.5
  7.1 0.0 copy-done.4
  7.1 8.0 %own_gram_first.1 = (f32[1296,80]{1,0:T(8,128)S(1)}, f32[1024,128]{1,0:T(8,128)S(1)}) custom-call(s32[1]{0:T(128)} %bitcast.turn_ref, s32[16]{0:T(128)S(1)} %copy-done.3, s32[16,2048]{1,0:T(8,128)S(1)} %copy-done.4, f32[16,2048]{1,0:T(8,128)S(1)} %copy-done.5, bf16[81,4096]{1,0:T(8,128)(2,1)S(1)} %copy-done.1), custom_call_target="tpu_custom_call" | custom-call | flops 8000000000 | bytes 8000000 | tf_op jit(solution)/shard_map/own_gram_first/pallas_call | solution.py:102
  15.0 10.1 %collective-permute-start.1 = (bf16[81,2048]{1,0:T(8,128)(2,1)S(1)}, bf16[81,2048]{1,0:T(8,128)(2,1)S(1)}, u32[]{:S(2)}, u32[]{:S(2)}) collective-permute-start(bf16[81,2048]{1,0:T(8,128)(2,1)S(1)} %get-tuple-element.18), channel_id=1, source_target_pairs={{8,0},{16,8},{24,16},{32,24},{40,32},{48,40},{56,48},{64,56},{72,6... | collective-permute-start | bytes 995336 | tf_op jit(solution)/shard_map/ppermute | solution.py:262
  25.1 0.5 %own_gram_second.1 = (f32[1296,80]{1,0:T(8,128)S(1)}, f32[1024,128]{1,0:T(8,128)S(1)}) custom-call(s32[1]{0:T(128)} %bitcast.turn_ref, s32[16]{0:T(128)S(1)} %copy-done.3, s32[16,2048]{1,0:T(8,128)S(1)} %copy-done.4, f32[16,2048]{1,0:T(8,128)S(1)} %copy-done.5, bf16[81,4096]{1,0:T(8,128)(2,1)S(1)} %copy-done.1, ...), custom_call_target="tpu_custom_call", output_to_operand_aliasing={{0}: (5, {}), {1}: (6, {})} | custom-call | flops 8000000000 | bytes 8000000 | tf_op jit(solution)/shard_map/own_gram_second/pallas_call | solution.py:102
  25.7 5.0 %collective-permute-done.lower_ref = bf16[81,2048]{1,0:T(8,128)(2,1)S(1)} collective-permute-done((bf16[81,2048]{1,0:T(8,128)(2,1)S(1)}, bf16[81,2048]{1,0:T(8,128)(2,1)S(1)}, u32[]{:S(2)}, u32[]{:S(2)}) %collective-permute-start) | collective-permute-done | bytes 331808 | tf_op jit(solution)/shard_map/ppermute | solution.py:259
  30.6 0.0 copy-start
  30.6 0.0 copy-start.2
  30.6 1.8 %lower_gram.1.own_ref = f32[1296,80]{1,0:T(8,128)S(1)} custom-call(f32[1296,80]{1,0:T(8,128)S(1)} %get-tuple-element.16.gram_in, f32[1024,128]{1,0:T(8,128)S(1)} %get-tuple-element.17.w_ref, bf16[81,2048]{1,0:T(8,128)(2,1)S(1)} %collective-permute-done.lower_ref), custom_call_target="tpu_custom_call", output_to_operand_aliasing={{}: (0, {})} | custom-call | flops 2000000000 | bytes 2000000 | tf_op jit(solution)/shard_map/lower_gram/pallas_call | solution.py:126
  32.5 0.0 collective-permute-done.1.upper_ref
  32.5 0.0 copy-done
  32.5 0.0 copy-done.2
  32.5 7.2 %finish.1 = bf16[16,80,512]{2,1,0:T(8,128)(2,1)} custom-call(s32[16]{0:T(128)S(1)} %copy-done.3, f32[1296,80]{1,0:T(8,128)S(1)} %lower_gram.1.own_ref, f32[1024,128]{1,0:T(8,128)S(1)} %get-tuple-element.17.w_ref, bf16[81,2048]{1,0:T(8,128)(2,1)S(1)} %collective-permute-done.1.upper_ref, bf16[16,80,512]{2,1,0:T(8,128)(2,1)S(1)} %copy-done, ...), custom_call_target="tpu_custom_call" | custom-call | tf_op jit(solution)/shard_map/finish/pallas_call | solution.py:236
Async XLA Ops:
  0.0 7.0 %copy-start.1 = (bf16[81,4096]{1,0:T(8,128)(2,1)S(1)}, bf16[81,4096]{1,0:T(8,128)(2,1)}, u32[]{:S(2)}) copy-start(bf16[81,4096]{1,0:T(8,128)(2,1)} %record.1) | copy-start | bytes 1990660
  0.0 7.0 %copy-start.3 = (s32[16]{0:T(128)S(1)}, s32[16]{0:T(128)}, u32[]{:S(2)}) copy-start(s32[16]{0:T(128)} %count_ref.1) | copy-start | bytes 196
  0.0 7.0 %copy-start.5 = (f32[16,2048]{1,0:T(8,128)S(1)}, f32[16,2048]{1,0:T(8,128)}, u32[]{:S(2)}) copy-start(f32[16,2048]{1,0:T(8,128)} %factor.1) | copy-start | bytes 393220
  0.0 7.0 %copy-start.4 = (s32[16,2048]{1,0:T(8,128)S(1)}, s32[16,2048]{1,0:T(8,128)}, u32[]{:S(2)}) copy-start(s32[16,2048]{1,0:T(8,128)} %index.1) | copy-start | bytes 393220
  1.2 29.4 %collective-permute-start = (bf16[81,2048]{1,0:T(8,128)(2,1)S(1)}, bf16[81,2048]{1,0:T(8,128)(2,1)S(1)}, u32[]{:S(2)}, u32[]{:S(2)}) collective-permute-start(bf16[81,2048]{1,0:T(8,128)(2,1)S(1)} %get-tuple-element.19), channel_id=1, source_target_pairs={{0,8},{8,16},{16,24},{24,32},{32,40},{40,48},{48,56},{56,64},{64,7... | collective-permute-start | bytes 995336 | tf_op jit(solution)/shard_map/ppermute | solution.py:259
  15.0 17.4 %collective-permute-start.1 = (bf16[81,2048]{1,0:T(8,128)(2,1)S(1)}, bf16[81,2048]{1,0:T(8,128)(2,1)S(1)}, u32[]{:S(2)}, u32[]{:S(2)}) collective-permute-start(bf16[81,2048]{1,0:T(8,128)(2,1)S(1)} %get-tuple-element.18), channel_id=1, source_target_pairs={{8,0},{16,8},{24,16},{32,24},{40,32},{48,40},{56,48},{64,56},{72,6... | collective-permute-start | bytes 995336 | tf_op jit(solution)/shard_map/ppermute | solution.py:262
  30.6 1.8 %copy-start = (bf16[16,80,512]{2,1,0:T(8,128)(2,1)S(1)}, bf16[16,80,512]{2,1,0:T(8,128)(2,1)}, u32[]{:S(2)}) copy-start(bf16[16,80,512]{2,1,0:T(8,128)(2,1)} %background_ref.1) | copy-start | bytes 3932164
  30.6 1.8 %copy-start.2 = (f32[16,512]{1,0:T(8,128)S(1)}, f32[16,512]{1,0:T(8,128)}, u32[]{:S(2)}) copy-start(f32[16,512]{1,0:T(8,128)} %mean_ref.1) | copy-start | bytes 98308

commit v6 on v5

--- a/solution.py
+++ b/solution.py
@@ -16,7 +16,7 @@
 F32 = jnp.float32
 NT = (((1,), (1,)), ((), ()))
 
-hist_unroll = 2
+hist_unroll = 8
 gram_chunk = 8
 
 
@@ -33,8 +33,8 @@
     lo_at = lax.broadcasted_iota(jnp.int32, (LANES, p_most), 0)
     hi_hot = jnp.where(hi_at == hi, factor, 0.0).astype(BF16)
     lo_hot = jnp.where(lo_at == lo, 1.0, 0.0).astype(BF16)
-    summed = lax.dot_general(hi_hot, lo_hot, NT, preferred_element_type=F32)
-    w_ref[pl.ds(block, groups, stride=blocks), :] = summed
+    summed = lax.dot_general(lo_hot, hi_hot, NT, preferred_element_type=F32)
+    w_ref[pl.ds(block, groups, stride=blocks), :] = summed.T
 
 
 def gram_part(record, w_ref, first, blocks):
@@ -66,7 +66,16 @@
     lax.fori_loop(0, record_ref.shape[1] // width, step, 0)
 
 
-def own_gram_body(count_ref, index_ref, factor_ref, record_ref, gram_ref, w_ref):
+def early():
+    return lax.axis_index("region") % RUN < 2
+
+
+def own_gram_body(
+    count_in, index_ref, factor_ref, record_ref, gram_ref, w_ref, active_ref, count_ref, sem
+):
+    copy = pltpu.make_async_copy(count_in, count_ref, sem)
+    copy.start()
+    copy.wait()
     blocks = index_ref.shape[0]
 
     def step(i, carry):
@@ -75,45 +84,49 @@
         return carry
 
     lax.fori_loop(0, blocks // hist_unroll, step, 0)
+    for b in range(blocks):
+        row = jnp.full((1, LANES), jnp.minimum(count_ref[b], 1), jnp.int32)
+        active_ref[b : b + 1, :] = row.astype(F32)
     gram_ref[...] = jnp.zeros_like(gram_ref)
     add_gram(record_ref, w_ref, HALO // LANES, blocks, gram_ref)
 
 
-def first_turn_kernel(turn_ref, *refs):
-    @pl.when(turn_ref[0] == 0)
+def first_turn_kernel(*refs):
+    @pl.when(early())
     def _():
         own_gram_body(*refs)
 
 
-def second_turn_kernel(turn_ref, count, index, factor, record, gram_in, w_in, gram_ref, w_ref):
-    del gram_in, w_in
-
-    @pl.when(turn_ref[0] != 0)
+def second_turn_kernel(count, index, factor, record, gram_in, w_in, active_in, *made):
+    del gram_in, w_in, active_in
+
+    @pl.when(jnp.logical_not(early()))
     def _():
-        own_gram_body(count, index, factor, record, gram_ref, w_ref)
-
-
-def own_gram(turn, obs_count, obs_index, localization, record, made=()):
-    blocks, p_most = obs_index.shape
+        own_gram_body(count, index, factor, record, *made)
+
+
+def own_gram(obs_count, obs_index, localization, record, made=()):
+    blocks = obs_index.shape[0]
     rows, columns = record.shape
     groups = (columns + 2 * HALO) // LANES
-    smem = pl.BlockSpec(memory_space=pltpu.SMEM)
     vmem = pl.BlockSpec(memory_space=pltpu.VMEM)
     return pl.pallas_call(
         second_turn_kernel if made else first_turn_kernel,
         out_shape=(
             jax.ShapeDtypeStruct((blocks * rows, rows - 1), F32),
             jax.ShapeDtypeStruct((groups * blocks, LANES), F32),
-        ),
-        in_specs=[smem, smem, vmem, vmem, vmem] + [vmem] * len(made),
-        out_specs=(vmem, vmem),
-        input_output_aliases={5: 0, 6: 1} if made else {},
+            jax.ShapeDtypeStruct((blocks, LANES), F32),
+        ),
+        in_specs=[vmem] * (4 + len(made)),
+        out_specs=(vmem,) * 3,
+        scratch_shapes=[pltpu.SMEM((blocks,), jnp.int32), pltpu.SemaphoreType.DMA],
+        input_output_aliases={4: 0, 5: 1, 6: 2} if made else {},
         compiler_params=pltpu.CompilerParams(vmem_limit_bytes=40 * 2**20),
         cost_estimate=pl.CostEstimate(
             flops=8_000_000_000, bytes_accessed=8_000_000, transcendentals=0
         ),
         name="own_gram_second" if made else "own_gram_first",
-    )(turn, obs_count, obs_index, localization, record, *made)
+    )(obs_count, obs_index, localization, record, *made)
 
 
 def lower_gram_kernel(gram_in, w_ref, lower_ref, gram_ref):
@@ -200,7 +213,7 @@
 
 
 def finish_kernel(
-    count_ref,
+    active_ref,
     own_ref,
     w_ref,
     upper_ref,
@@ -221,7 +234,7 @@
     solved, eye = solve_blocks(informations, innovations)
     copies = []
     for b in range(blocks):
-        weights = jnp.where(count_ref[b] > 0, solved[b], eye).astype(BF16)
+        weights = jnp.where(active_ref[b : b + 1, :members] > 0.5, solved[b], eye).astype(BF16)
         mixed = jnp.dot(weights, background_ref[b], preferred_element_type=F32)
         made_ref[b] = (mean_ref[b : b + 1, :] + mixed).astype(BF16)
         copies.append(pltpu.make_async_copy(made_ref.at[b], out_ref.at[b], sems.at[b]))
@@ -230,13 +243,13 @@
         copy.wait()
 
 
-def finish(obs_count, own, w, upper, background, background_mean):
+def finish(active, own, w, upper, background, background_mean):
     blocks = background.shape[0]
     vmem = pl.BlockSpec(memory_space=pltpu.VMEM)
     return pl.pallas_call(
         finish_kernel,
         out_shape=jax.ShapeDtypeStruct(background.shape, BF16),
-        in_specs=[pl.BlockSpec(memory_space=pltpu.SMEM)] + [vmem] * 5,
+        in_specs=[vmem] * 6,
         out_specs=pl.BlockSpec(memory_space=pl.ANY),
         scratch_shapes=[
             pltpu.VMEM(own.shape, F32),
@@ -245,7 +258,7 @@
         ],
         compiler_params=pltpu.CompilerParams(vmem_limit_bytes=40 * 2**20),
         name="finish",
-    )(obs_count, own, w, upper, background, background_mean)
+    )(active, own, w, upper, background, background_mean)
 
 
 def on_device(observations, obs_index, obs_count, localization, background, background_mean):
@@ -253,16 +266,14 @@
     up = [(i, (i + 1) % count) for i in range(count)]
     down = [(j, i) for i, j in up]
     own_columns = observations.shape[1]
-    place = lax.axis_index("region")
-    turn = jnp.minimum(place % RUN // 2, 1).astype(jnp.int32)[None]
-    given = (turn, obs_count, obs_index, localization, observations)
+    given = (obs_count, obs_index, localization, observations)
     lower = lax.ppermute(observations[:, own_columns - HALO :], "region", up)
     made = own_gram(*given)
-    first, *made = lax.optimization_barrier((observations[:, :HALO], *made))
-    upper = lax.ppermute(first, "region", down)
-    own, w = own_gram(*given, made)
+    below, *made = lax.optimization_barrier((observations[:, :HALO], *made))
+    upper = lax.ppermute(below, "region", down)
+    own, w, active = own_gram(*given, made)
     own = lower_gram(own, w, lower)
-    return finish(obs_count, own, w, upper, background, background_mean)
+    return finish(active, own, w, upper, background, background_mean)
 
 
 def solution(mesh):

time: 39.8 us -> 39.3 us (0.987)
  Pallas kernels: 17.5 us -> 15.1 us
  waiting for transfers between devices: 4.97 us -> 6.04 us
  starting transfers between devices: 15.8 us -> 16.6 us
    pallas_call x2, Pallas kernels: 8.52 us -> 6.72 us  [own_gram(): pl.pallas_call(second_turn_kernel if made else first_turn_kernel, out_sha...]
    ppermute x1, waiting for transfers between devices: 4.97 us -> 6.04 us  [on_device(): lower = lax.ppermute(observations[:, own_columns - HALO:], 'region', up)]
    ppermute x1, starting transfers between devices: 10.1 us -> 10.8 us  [on_device(): upper = lax.ppermute(below, 'region', down)]
    pallas_call x1, Pallas kernels: 7.18 us -> 6.62 us  [finish(): pl.pallas_call(finish_kernel, out_shape=jax.ShapeDtypeStruct(background.s...]
  transfers between devices with their start and end apart: 2 -> 2, of which waited for: 1 -> 1; matrix products, arithmetic and copies ran while one was open for 0% -> 0% of each run, Pallas kernels for 26% -> 22%
where the time goes in v6:
time: 39.3 us; the launch traced here: 39.1 us
  starting transfers between devices  16.6 us (42%)
  Pallas kernels  15.1 us (38%)
  waiting for transfers between devices  6.04 us (15%)
  local copies, waits for them, and re-layouts  1.25 us (3%)
    ppermute x1, starting transfers between devices, on_device(): upper = lax.ppermute(below, 'region', down)  10.8 us
    pallas_call x2, Pallas kernels, own_gram(): pl.pallas_call(second_turn_kernel if made else first_turn_kernel, out_sha...  6.72 us
    pallas_call x1, Pallas kernels, finish(): pl.pallas_call(finish_kernel, out_shape=jax.ShapeDtypeStruct(background.s...  6.62 us
    ppermute x1, waiting for transfers between devices, on_device(): lower = lax.ppermute(observations[:, own_columns - HALO:], 'region', up)  6.04 us
    ppermute x1, starting transfers between devices, on_device(): lower = lax.ppermute(observations[:, own_columns - HALO:], 'region', up)  5.74 us
    pallas_call x1, Pallas kernels, lower_gram(): pl.pallas_call(lower_gram_kernel, out_shape=jax.ShapeDtypeStruct(own.shap...  1.81 us
    slice x1, local copies, waits for them, and re-layouts, on_device(): lower = lax.ppermute(observations[:, own_columns - HALO:], 'region', up)  1.23 us
  transfers between devices with their start and end apart: 2, of which 1 were waited for; matrix products, arithmetic and copies ran while one was open for 0% of the time, Pallas kernels for 22%

profile of v6, /device:TPU:1, one launch (start us, length us, event | category | flops | bytes accessed | tf_op | source)
XLA Modules:
  0.0 39.1 jit_solution(13588480682676460137)
XLA Ops:
  0.0 0.0 copy-start.1
  0.0 0.0 copy-start.4
  0.0 0.0 copy-start.5
  0.0 0.0 copy-start.3
  0.0 1.2 %fusion = (bf16[81,2048]{1,0:T(8,128)(2,1)S(1)}, bf16[81,2048]{1,0:T(8,128)(2,1)S(1)}) fusion(bf16[81,4096]{1,0:T(8,128)(2,1)} %record.1), kind=kLoop, calls=%fused_computation | loop fusion | bytes 1327104 | tf_op jit(solution)/shard_map/slice | solution.py:270
  1.3 5.7 %collective-permute-start = (bf16[81,2048]{1,0:T(8,128)(2,1)S(1)}, bf16[81,2048]{1,0:T(8,128)(2,1)S(1)}, u32[]{:S(2)}, u32[]{:S(2)}) collective-permute-start(bf16[81,2048]{1,0:T(8,128)(2,1)S(1)} %get-tuple-element.25), channel_id=1, source_target_pairs={{0,8},{8,16},{16,24},{24,32},{32,40},{40,48},{48,56},{56,64},{64,7... | collective-permute-start | bytes 995336 | tf_op jit(solution)/shard_map/ppermute | solution.py:270
  7.0 0.0 copy-done.1
  7.0 0.0 copy-done.4
  7.0 0.0 copy-done.5
  7.0 0.0 copy-done.3
  7.0 6.7 %own_gram_first.1 = (f32[1296,80]{1,0:T(8,128)S(1)}, f32[1024,128]{1,0:T(8,128)S(1)}, f32[16,128]{1,0:T(8,128)S(1)}) custom-call(s32[16]{0:T(128)S(1)} %copy-done.5, s32[16,2048]{1,0:T(8,128)S(1)} %copy-done.3, f32[16,2048]{1,0:T(8,128)S(1)} %copy-done.4, bf16[81,4096]{1,0:T(8,128)(2,1)S(1)} %copy-done.1), custom_call_target="tpu_custom_call" | custom-call | flops 8000000000 | bytes 8000000 | tf_op jit(solution)/shard_map/own_gram_first/pallas_call | solution.py:113
  13.7 10.8 %collective-permute-start.1 = (bf16[81,2048]{1,0:T(8,128)(2,1)S(1)}, bf16[81,2048]{1,0:T(8,128)(2,1)S(1)}, u32[]{:S(2)}, u32[]{:S(2)}) collective-permute-start(bf16[81,2048]{1,0:T(8,128)(2,1)S(1)} %get-tuple-element.24), channel_id=1, source_target_pairs={{8,0},{16,8},{24,16},{32,24},{40,32},{48,40},{56,48},{64,56},{72,6... | collective-permute-start | bytes 995336 | tf_op jit(solution)/shard_map/ppermute | solution.py:273
  24.6 6.0 %collective-permute-done.lower_ref = bf16[81,2048]{1,0:T(8,128)(2,1)S(1)} collective-permute-done((bf16[81,2048]{1,0:T(8,128)(2,1)S(1)}, bf16[81,2048]{1,0:T(8,128)(2,1)S(1)}, u32[]{:S(2)}, u32[]{:S(2)}) %collective-permute-start) | collective-permute-done | bytes 331808 | tf_op jit(solution)/shard_map/ppermute | solution.py:270
  30.6 0.0 copy-start
  30.6 0.0 copy-start.2
  30.6 1.8 %lower_gram.1.own_ref = f32[1296,80]{1,0:T(8,128)S(1)} custom-call(f32[1296,80]{1,0:T(8,128)S(1)} %get-tuple-element.22.gram_in, f32[1024,128]{1,0:T(8,128)S(1)} %get-tuple-element.23.w_ref, bf16[81,2048]{1,0:T(8,128)(2,1)S(1)} %collective-permute-done.lower_ref), custom_call_target="tpu_custom_call", output_to_operand_aliasing={{}: (0, {})} | custom-call | flops 2000000000 | bytes 2000000 | tf_op jit(solution)/shard_map/lower_gram/pallas_call | solution.py:139
  32.5 0.0 collective-permute-done.1.upper_ref
  32.5 0.0 copy-done
  32.5 0.0 copy-done.2
  32.5 6.6 %finish.1 = bf16[16,80,512]{2,1,0:T(8,128)(2,1)} custom-call(f32[16,128]{1,0:T(8,128)S(1)} %get-tuple-element.21.active_ref, f32[1296,80]{1,0:T(8,128)S(1)} %lower_gram.1.own_ref, f32[1024,128]{1,0:T(8,128)S(1)} %get-tuple-element.23.w_ref, bf16[81,2048]{1,0:T(8,128)(2,1)S(1)} %collective-permute-done.1.upper_ref, bf16[16,80,512]{2,1,0:T(8,128)(2,1)S(1)} %copy-done, ...), custom_call_target="tpu_custom_call" | custom-call | tf_op jit(solution)/shard_map/finish/pallas_call | solution.py:249
  (1 shorter events, 0.0 us)
Async XLA Ops:
  0.0 7.0 %copy-start.1 = (bf16[81,4096]{1,0:T(8,128)(2,1)S(1)}, bf16[81,4096]{1,0:T(8,128)(2,1)}, u32[]{:S(2)}) copy-start(bf16[81,4096]{1,0:T(8,128)(2,1)} %record.1) | copy-start | bytes 1990660
  0.0 7.0 %copy-start.4 = (f32[16,2048]{1,0:T(8,128)S(1)}, f32[16,2048]{1,0:T(8,128)}, u32[]{:S(2)}) copy-start(f32[16,2048]{1,0:T(8,128)} %factor.1) | copy-start | bytes 393220
  0.0 7.0 %copy-start.5 = (s32[16]{0:T(128)S(1)}, s32[16]{0:T(128)}, u32[]{:S(2)}) copy-start(s32[16]{0:T(128)} %count.1) | copy-start | bytes 196
  0.0 7.0 %copy-start.3 = (s32[16,2048]{1,0:T(8,128)S(1)}, s32[16,2048]{1,0:T(8,128)}, u32[]{:S(2)}) copy-start(s32[16,2048]{1,0:T(8,128)} %index.1) | copy-start | bytes 393220
  1.3 29.4 %collective-permute-start = (bf16[81,2048]{1,0:T(8,128)(2,1)S(1)}, bf16[81,2048]{1,0:T(8,128)(2,1)S(1)}, u32[]{:S(2)}, u32[]{:S(2)}) collective-permute-start(bf16[81,2048]{1,0:T(8,128)(2,1)S(1)} %get-tuple-element.25), channel_id=1, source_target_pairs={{0,8},{8,16},{16,24},{24,32},{32,40},{40,48},{48,56},{56,64},{64,7... | collective-permute-start | bytes 995336 | tf_op jit(solution)/shard_map/ppermute | solution.py:270
  13.7 18.7 %collective-permute-start.1 = (bf16[81,2048]{1,0:T(8,128)(2,1)S(1)}, bf16[81,2048]{1,0:T(8,128)(2,1)S(1)}, u32[]{:S(2)}, u32[]{:S(2)}) collective-permute-start(bf16[81,2048]{1,0:T(8,128)(2,1)S(1)} %get-tuple-element.24), channel_id=1, source_target_pairs={{8,0},{16,8},{24,16},{32,24},{40,32},{48,40},{56,48},{64,56},{72,6... | collective-permute-start | bytes 995336 | tf_op jit(solution)/shard_map/ppermute | solution.py:273
  30.6 1.8 %copy-start = (bf16[16,80,512]{2,1,0:T(8,128)(2,1)S(1)}, bf16[16,80,512]{2,1,0:T(8,128)(2,1)}, u32[]{:S(2)}) copy-start(bf16[16,80,512]{2,1,0:T(8,128)(2,1)} %background_ref.1) | copy-start | bytes 3932164
  30.6 1.8 %copy-start.2 = (f32[16,512]{1,0:T(8,128)S(1)}, f32[16,512]{1,0:T(8,128)}, u32[]{:S(2)}) copy-start(f32[16,512]{1,0:T(8,128)} %mean_ref.1) | copy-start | bytes 98308

commit v7 on v6

--- a/solution.py
+++ b/solution.py
@@ -130,8 +130,8 @@
 
 
 def lower_gram_kernel(gram_in, w_ref, lower_ref, gram_ref):
-    gram_ref[...] = gram_in[...]
-    add_gram(lower_ref, w_ref, 0, gram_in.shape[0] // lower_ref.shape[0], gram_ref)
+    blocks = gram_in.shape[0] // lower_ref.shape[0]
+    gram_ref[...] = gram_in[...] + gram_part(lower_ref[...], w_ref, 0, blocks)
 
 
 def lower_gram(own, w, lower):
@@ -226,8 +226,8 @@
 ):
     blocks, members, _ = background_ref.shape
     groups = w_ref.shape[0] // blocks
-    gram_ref[...] = own_ref[...]
-    add_gram(upper_ref, w_ref, groups - HALO // LANES, blocks, gram_ref)
+    upper = gram_part(upper_ref[...], w_ref, groups - HALO // LANES, blocks)
+    gram_ref[...] = own_ref[...] + upper
     informations = [gram_ref[b * members : (b + 1) * members, :] for b in range(blocks)]
     at = blocks * members
     innovations = [gram_ref[at + b : at + b + 1, :] for b in range(blocks)]

time: 39.3 us -> 39.1 us (level)
  transfers between devices with their start and end apart: 2 -> 2, of which waited for: 1 -> 1; matrix products, arithmetic and copies ran while one was open for 0% -> 0% of each run, Pallas kernels for 22% -> 21%
where the time goes in v7:
time: 39.1 us; the launch traced here: 38.9 us
  starting transfers between devices  16.6 us (42%)
  Pallas kernels  14.9 us (38%)
  waiting for transfers between devices  6.04 us (15%)
  local copies, waits for them, and re-layouts  1.25 us (3%)
    ppermute x1, starting transfers between devices, on_device(): upper = lax.ppermute(below, 'region', down)  10.8 us
    pallas_call x2, Pallas kernels, own_gram(): pl.pallas_call(second_turn_kernel if made else first_turn_kernel, out_sha...  6.72 us
    pallas_call x1, Pallas kernels, finish(): pl.pallas_call(finish_kernel, out_shape=jax.ShapeDtypeStruct(background.s...  6.61 us
    ppermute x1, waiting for transfers between devices, on_device(): lower = lax.ppermute(observations[:, own_columns - HALO:], 'region', up)  6.04 us
    ppermute x1, starting transfers between devices, on_device(): lower = lax.ppermute(observations[:, own_columns - HALO:], 'region', up)  5.74 us
    pallas_call x1, Pallas kernels, lower_gram(): pl.pallas_call(lower_gram_kernel, out_shape=jax.ShapeDtypeStruct(own.shap...  1.62 us
    slice x1, local copies, waits for them, and re-layouts, on_device(): lower = lax.ppermute(observations[:, own_columns - HALO:], 'region', up)  1.23 us
  transfers between devices with their start and end apart: 2, of which 1 were waited for; matrix products, arithmetic and copies ran while one was open for 0% of the time, Pallas kernels for 21%

profile of v7, /device:TPU:1, one launch (start us, length us, event | category | flops | bytes accessed | tf_op | source)
XLA Modules:
  0.0 38.9 jit_solution(5456356502811784403)
XLA Ops:
  0.0 0.0 copy-start.1
  0.0 0.0 copy-start.4
  0.0 0.0 copy-start.5
  0.0 0.0 copy-start.3
  0.0 1.2 %fusion = (bf16[81,2048]{1,0:T(8,128)(2,1)S(1)}, bf16[81,2048]{1,0:T(8,128)(2,1)S(1)}) fusion(bf16[81,4096]{1,0:T(8,128)(2,1)} %record.1), kind=kLoop, calls=%fused_computation | loop fusion | bytes 1327104 | tf_op jit(solution)/shard_map/slice | solution.py:270
  1.3 5.7 %collective-permute-start = (bf16[81,2048]{1,0:T(8,128)(2,1)S(1)}, bf16[81,2048]{1,0:T(8,128)(2,1)S(1)}, u32[]{:S(2)}, u32[]{:S(2)}) collective-permute-start(bf16[81,2048]{1,0:T(8,128)(2,1)S(1)} %get-tuple-element.25), channel_id=1, source_target_pairs={{0,8},{8,16},{16,24},{24,32},{32,40},{40,48},{48,56},{56,64},{64,7... | collective-permute-start | bytes 995336 | tf_op jit(solution)/shard_map/ppermute | solution.py:270
  7.0 0.0 copy-done.1
  7.0 0.0 copy-done.4
  7.0 0.0 copy-done.5
  7.0 0.0 copy-done.3
  7.0 6.7 %own_gram_first.1 = (f32[1296,80]{1,0:T(8,128)S(1)}, f32[1024,128]{1,0:T(8,128)S(1)}, f32[16,128]{1,0:T(8,128)S(1)}) custom-call(s32[16]{0:T(128)S(1)} %copy-done.5, s32[16,2048]{1,0:T(8,128)S(1)} %copy-done.3, f32[16,2048]{1,0:T(8,128)S(1)} %copy-done.4, bf16[81,4096]{1,0:T(8,128)(2,1)S(1)} %copy-done.1), custom_call_target="tpu_custom_call" | custom-call | flops 8000000000 | bytes 8000000 | tf_op jit(solution)/shard_map/own_gram_first/pallas_call | solution.py:113
  13.7 10.8 %collective-permute-start.1 = (bf16[81,2048]{1,0:T(8,128)(2,1)S(1)}, bf16[81,2048]{1,0:T(8,128)(2,1)S(1)}, u32[]{:S(2)}, u32[]{:S(2)}) collective-permute-start(bf16[81,2048]{1,0:T(8,128)(2,1)S(1)} %get-tuple-element.24), channel_id=1, source_target_pairs={{8,0},{16,8},{24,16},{32,24},{40,32},{48,40},{56,48},{64,56},{72,6... | collective-permute-start | bytes 995336 | tf_op jit(solution)/shard_map/ppermute | solution.py:273
  24.6 6.0 %collective-permute-done.lower_ref = bf16[81,2048]{1,0:T(8,128)(2,1)S(1)} collective-permute-done((bf16[81,2048]{1,0:T(8,128)(2,1)S(1)}, bf16[81,2048]{1,0:T(8,128)(2,1)S(1)}, u32[]{:S(2)}, u32[]{:S(2)}) %collective-permute-start) | collective-permute-done | bytes 331808 | tf_op jit(solution)/shard_map/ppermute | solution.py:270
  30.6 0.0 copy-start
  30.6 0.0 copy-start.2
  30.6 1.6 %lower_gram.1.own_ref = f32[1296,80]{1,0:T(8,128)S(1)} custom-call(f32[1296,80]{1,0:T(8,128)S(1)} %get-tuple-element.22.gram_in, f32[1024,128]{1,0:T(8,128)S(1)} %get-tuple-element.23.w_ref, bf16[81,2048]{1,0:T(8,128)(2,1)S(1)} %collective-permute-done.lower_ref), custom_call_target="tpu_custom_call", output_to_operand_aliasing={{}: (0, {})} | custom-call | flops 2000000000 | bytes 2000000 | tf_op jit(solution)/shard_map/lower_gram/pallas_call | solution.py:139
  32.3 0.0 collective-permute-done.1.upper_ref
  32.3 0.0 copy-done
  32.3 0.0 copy-done.2
  32.3 6.6 %finish.1 = bf16[16,80,512]{2,1,0:T(8,128)(2,1)} custom-call(f32[16,128]{1,0:T(8,128)S(1)} %get-tuple-element.21.active_ref, f32[1296,80]{1,0:T(8,128)S(1)} %lower_gram.1.own_ref, f32[1024,128]{1,0:T(8,128)S(1)} %get-tuple-element.23.w_ref, bf16[81,2048]{1,0:T(8,128)(2,1)S(1)} %collective-permute-done.1.upper_ref, bf16[16,80,512]{2,1,0:T(8,128)(2,1)S(1)} %copy-done, ...), custom_call_target="tpu_custom_call" | custom-call | tf_op jit(solution)/shard_map/finish/pallas_call | solution.py:249
  (1 shorter events, 0.0 us)
Async XLA Ops:
  0.0 7.0 %copy-start.1 = (bf16[81,4096]{1,0:T(8,128)(2,1)S(1)}, bf16[81,4096]{1,0:T(8,128)(2,1)}, u32[]{:S(2)}) copy-start(bf16[81,4096]{1,0:T(8,128)(2,1)} %record.1) | copy-start | bytes 1990660
  0.0 7.0 %copy-start.4 = (f32[16,2048]{1,0:T(8,128)S(1)}, f32[16,2048]{1,0:T(8,128)}, u32[]{:S(2)}) copy-start(f32[16,2048]{1,0:T(8,128)} %factor.1) | copy-start | bytes 393220
  0.0 7.0 %copy-start.5 = (s32[16]{0:T(128)S(1)}, s32[16]{0:T(128)}, u32[]{:S(2)}) copy-start(s32[16]{0:T(128)} %count.1) | copy-start | bytes 196
  0.0 7.0 %copy-start.3 = (s32[16,2048]{1,0:T(8,128)S(1)}, s32[16,2048]{1,0:T(8,128)}, u32[]{:S(2)}) copy-start(s32[16,2048]{1,0:T(8,128)} %index.1) | copy-start | bytes 393220
  1.3 29.4 %collective-permute-start = (bf16[81,2048]{1,0:T(8,128)(2,1)S(1)}, bf16[81,2048]{1,0:T(8,128)(2,1)S(1)}, u32[]{:S(2)}, u32[]{:S(2)}) collective-permute-start(bf16[81,2048]{1,0:T(8,128)(2,1)S(1)} %get-tuple-element.25), channel_id=1, source_target_pairs={{0,8},{8,16},{16,24},{24,32},{32,40},{40,48},{48,56},{56,64},{64,7... | collective-permute-start | bytes 995336 | tf_op jit(solution)/shard_map/ppermute | solution.py:270
  13.7 18.5 %collective-permute-start.1 = (bf16[81,2048]{1,0:T(8,128)(2,1)S(1)}, bf16[81,2048]{1,0:T(8,128)(2,1)S(1)}, u32[]{:S(2)}, u32[]{:S(2)}) collective-permute-start(bf16[81,2048]{1,0:T(8,128)(2,1)S(1)} %get-tuple-element.24), channel_id=1, source_target_pairs={{8,0},{16,8},{24,16},{32,24},{40,32},{48,40},{56,48},{64,56},{72,6... | collective-permute-start | bytes 995336 | tf_op jit(solution)/shard_map/ppermute | solution.py:273
  30.6 1.6 %copy-start = (bf16[16,80,512]{2,1,0:T(8,128)(2,1)S(1)}, bf16[16,80,512]{2,1,0:T(8,128)(2,1)}, u32[]{:S(2)}) copy-start(bf16[16,80,512]{2,1,0:T(8,128)(2,1)} %background_ref.1) | copy-start | bytes 3932164
  30.6 1.7 %copy-start.2 = (f32[16,512]{1,0:T(8,128)S(1)}, f32[16,512]{1,0:T(8,128)}, u32[]{:S(2)}) copy-start(f32[16,512]{1,0:T(8,128)} %mean_ref.1) | copy-start | bytes 98308
